TPU v7x, 512 devices: a whole 4x8x8 slice. The times are simulated.
512 devices in a mesh: row: 128 (over y, z, core), col: 4 (over x).
Axes of the slice: x: 4, y: 8, z: 8, core: 2. Of those that a mesh axis runs over, the one named last changes fastest.
Arguments:
- rhs: float32 [2, 128, 1024, 128], P(None, 'row'), may hold values from -6 to 6
- diag_inv: bfloat16 [4, 1024, 1024], P(None, 'row'), as said below
- blocks: bfloat16 [1, 4, 128, 1, 1024, 1024], P(None, 'col', 'row'), may hold values from -0.09375 to 0.09375
- block_rows: int32 [1, 4, 128, 1], P(None, 'col', 'row'), may hold values from 0 to 1, as said below
- counts: int32 [1, 4, 128], P(None, 'col', 'row'), may hold values from 0 to 1, as said below
Outputs:
- solved: float32 [1, 4, 1024, 128], P(None, 'col')
- remainder: float32 [2, 128, 1024, 128], P(None, 'row')
Inputs may be any that keep to these rules, and one draw needn't show every extreme that they name: `diag_inv`: lower triangular. `block_rows`: the 1 entries of one list are different; for row indices r below 4, slot 0 lists local block row 0. `counts`: 1 is reached in every draw; for row indices r below 4 the count is 1.
All inputs are finite; a program needn't handle non-finite values.
Results may differ from a plain program's by a relative error of at most 0.0041.
Values may be sent and summed in bfloat16 or wider, within the bound.
A program may use at most 64 MiB of HBM per device.

v0:
```python
import jax
import jax.numpy as jnp
from jax import lax
from jax.sharding import PartitionSpec as P


def broadcast(value, axis, root):
    mine = lax.axis_index(axis) == root
    return lax.psum(jnp.where(mine, value, jnp.zeros_like(value)), axis)


def on_device(rhs, diag_inv, blocks, block_rows, counts):
    nrow = lax.axis_size("row")
    ncol = lax.axis_size("col")
    my_row = lax.axis_index("row")
    my_col = lax.axis_index("col")
    kc = diag_inv.shape[0]
    rb_local = rhs.shape[0]
    nz_local = blocks.shape[3]
    local_rhs = rhs[:, 0]
    partial_value = jnp.zeros(local_rhs.shape, jnp.float32)
    solved_list = [jnp.zeros(local_rhs.shape[1:], jnp.float32)]
    slot_ids = jnp.arange(nz_local, dtype=jnp.int32)
    local_ids = jnp.arange(rb_local, dtype=jnp.int32)
    for k in range(kc):
        j = k // ncol
        owner_row = k % nrow
        local_pivot = k // nrow
        mine_row = my_row == owner_row
        mine_col = my_col == k % ncol
        pivot_part = jnp.where(mine_row, partial_value[local_pivot], jnp.float32(0.0))
        summed = lax.psum(pivot_part, "col")
        updated = (local_rhs[local_pivot] - summed).astype(jnp.bfloat16)
        pivot_bf = broadcast(updated, "row", owner_row)
        row_part = jnp.dot(diag_inv[k], pivot_bf, preferred_element_type=jnp.float32)
        sol = lax.all_gather(row_part, "row", axis=0, tiled=True)
        sol_bf = sol.astype(jnp.bfloat16)
        rows = block_rows[j, 0, 0]
        glob = rows * nrow + my_row
        valid = (slot_ids < counts[j, 0, 0]) & (glob > k) & mine_col
        weights = (valid[:, None] & (rows[:, None] == local_ids[None, :])).astype(jnp.float32)
        contrib = jnp.einsum(
            "sab,bn->san", blocks[j, 0, 0], sol_bf, preferred_element_type=jnp.float32
        )
        partial_value = partial_value + jnp.einsum(
            "sl,san->lan", weights, contrib, precision=lax.Precision.HIGHEST
        )
        solved_list[j] = jnp.where(mine_col, sol, solved_list[j])
    total = lax.psum(partial_value, "col")
    remainder = (local_rhs - total)[:, None]
    solved = jnp.stack(solved_list)[:, None]
    return (solved, remainder)


def solution(mesh):
    in_specs = (
        P(None, "row", None, None),
        P(None, "row", None),
        P(None, "col", "row", None, None, None),
        P(None, "col", "row", None),
        P(None, "col", "row"),
    )
    out_specs = (P(None, "col", None, None), P(None, "row", None, None))
    return jax.shard_map(
        on_device, mesh=mesh, in_specs=in_specs, out_specs=out_specs, check_vma=False
    )
```

profile of v0, /device:TPU:9, one launch (start us, length us, event | category | flops | bytes accessed | tf_op | source)
XLA Modules:
  0.0 1226.0 jit_solution(898332599292203441)
XLA Ops:
  7.2 1.9 fusion.30
  10.5 194.9 %all-reduce.9.cloned.1.call-done = bf16[1024,128]{1,0:T(8,128)(2,1)} async-done(((bf16[1024,128]{1,0:T(8,128)(2,1)}), bf16[1024,128]{1,0:T(8,128)(2,1)}) %all-reduce.9.cloned.1.call-update) | async-done | bytes 262160 | tf_op jit(solution)/shard_map/psum | solution.py:9
  205.5 1.1 convolution_bitcast_fusion.3
  206.6 48.8 %all_gather.12 = f32[1024,128]{1,0:T(8,128)S(1)} all-gather(f32[8,128]{1,0:T(8,128)S(1)} %convolution_bitcast_fusion.3), channel_id=1, replica_groups=mesh['row'=128,'col'=4] {'row'}, dimensions={0}, use_global_device_ids=true | all-gather | bytes 528384 | tf_op jit(solution)/shard_map/all_gather | solution.py:36
  258.3 50.0 %all-reduce.11.cloned.1.call-done = f32[1024,128]{1,0:T(8,128)} async-done(((f32[1024,128]{1,0:T(8,128)}), f32[1024,128]{1,0:T(8,128)}) %all-reduce.11.cloned.1.call-update) | async-done | bytes 524304 | tf_op jit(solution)/shard_map/psum | solution.py:32
  308.2 2.0 fusion.29
  310.3 193.5 %all-reduce.13.cloned.1.call-done = bf16[1024,128]{1,0:T(8,128)(2,1)} async-done(((bf16[1024,128]{1,0:T(8,128)(2,1)}), bf16[1024,128]{1,0:T(8,128)(2,1)}) %all-reduce.13.cloned.1.call-update) | async-done | bytes 262160 | tf_op jit(solution)/shard_map/psum | solution.py:9
  503.8 1.1 convolution_bitcast_fusion.2
  504.9 48.8 %all_gather.13 = f32[1024,128]{1,0:T(8,128)S(1)} all-gather(f32[8,128]{1,0:T(8,128)S(1)} %convolution_bitcast_fusion.2), channel_id=1, replica_groups=mesh['row'=128,'col'=4] {'row'}, dimensions={0}, use_global_device_ids=true | all-gather | bytes 528384 | tf_op jit(solution)/shard_map/all_gather | solution.py:36
  554.5 1.6 fusion.11
  556.2 1.2 copy.8
  557.6 0.8 fusion.22
  558.5 50.0 %all-reduce.15.cloned.1.call-done = f32[1024,128]{1,0:T(8,128)} async-done(((f32[1024,128]{1,0:T(8,128)}), f32[1024,128]{1,0:T(8,128)}) %all-reduce.15.cloned.1.call-update) | async-done | bytes 524304 | tf_op jit(solution)/shard_map/psum | solution.py:32
  608.5 2.0 fusion.28
  610.5 193.3 %all-reduce.17.cloned.1.call-done = bf16[1024,128]{1,0:T(8,128)(2,1)} async-done(((bf16[1024,128]{1,0:T(8,128)(2,1)}), bf16[1024,128]{1,0:T(8,128)(2,1)}) %all-reduce.17.cloned.1.call-update) | async-done | bytes 262160 | tf_op jit(solution)/shard_map/psum | solution.py:9
  803.9 1.1 convolution_bitcast_fusion.1
  805.0 48.8 %all_gather.14 = f32[1024,128]{1,0:T(8,128)S(1)} all-gather(f32[8,128]{1,0:T(8,128)S(1)} %convolution_bitcast_fusion.1), channel_id=1, replica_groups=mesh['row'=128,'col'=4] {'row'}, dimensions={0}, use_global_device_ids=true | all-gather | bytes 528384 | tf_op jit(solution)/shard_map/all_gather | solution.py:36
  854.6 1.6 fusion.14
  856.2 2.0 copy.9
  858.3 1.3 multiply_add_fusion.1
  859.6 0.8 fusion.21
  860.5 50.0 %all-reduce.19.cloned.1.call-done = f32[1024,128]{1,0:T(8,128)} async-done(((f32[1024,128]{1,0:T(8,128)}), f32[1024,128]{1,0:T(8,128)}) %all-reduce.19.cloned.1.call-update) | async-done | bytes 524304 | tf_op jit(solution)/shard_map/psum | solution.py:32
  910.4 2.0 fusion.27
  912.5 193.5 %all-reduce.21.cloned.1.call-done = bf16[1024,128]{1,0:T(8,128)(2,1)} async-done(((bf16[1024,128]{1,0:T(8,128)(2,1)}), bf16[1024,128]{1,0:T(8,128)(2,1)}) %all-reduce.21.cloned.1.call-update) | async-done | bytes 262160 | tf_op jit(solution)/shard_map/psum | solution.py:9
  1106.0 1.1 convolution_bitcast_fusion
  1107.1 49.0 %all_gather.15 = f32[1024,128]{1,0:T(8,128)S(1)} all-gather(f32[8,128]{1,0:T(8,128)S(1)} %convolution_bitcast_fusion), channel_id=1, replica_groups=mesh['row'=128,'col'=4] {'row'}, dimensions={0}, use_global_device_ids=true | all-gather | bytes 528384 | tf_op jit(solution)/shard_map/all_gather | solution.py:36
  1156.9 1.6 fusion.17
  1158.5 2.0 copy.10
  1160.5 2.5 multiply_add_fusion
  1163.0 2.0 select_bitcast_fusion
  1165.0 51.5 %all-reduce.23.cloned.1.call-done = f32[2,1024,128]{2,1,0:T(8,128)} async-done(((f32[2,1024,128]{2,1,0:T(8,128)}), f32[2,1024,128]{2,1,0:T(8,128)}) %all-reduce.23.cloned.1.call-update) | async-done | bytes 1048592 | tf_op jit(solution)/shard_map/psum | solution.py:49
  1216.5 2.6 fusion.20
  (37 shorter events, 5.9 us)
Async XLA Ops:
  7.2 249.0 %copy-start = (bf16[1,1,1,1,1024,1024]{5,4,3,2,1,0:T(8,128)(2,1)S(1)}, bf16[1,1,1,1,1024,1024]{5,4,3,2,1,0:T(8,128)(2,1)}, u32[]{:S(2)}) copy-start(bf16[1,1,1,1,1024,1024]{5,4,3,2,1,0:T(8,128)(2,1)} %param.7) | copy-start | bytes 6291460
  7.2 198.3 %all-reduce.9.cloned.1.call-start = ((), (), s32[]{:S(2)}) async-start(), calls=%async_computation | async-start | bytes 524288 | tf_op jit(solution)/shard_map/psum | solution.py:9
  9.2 299.1 %all-reduce.11.cloned.1.call-start = ((), (), s32[]{:S(2)}) async-start(), calls=%async_computation.1 | async-start | bytes 1048576 | tf_op jit(solution)/shard_map/psum | solution.py:32
  255.4 0.8 copy-start.1
  257.2 246.6 %copy-start.5 = (bf16[4,8,1024]{2,1,0:T(8,128)(2,1)S(1)}, bf16[4,8,1024]{2,1,0:T(8,128)(2,1)}, u32[]{:S(2)}) copy-start(bf16[4,8,1024]{2,1,0:T(8,128)(2,1)} %param.6) | copy-start | bytes 196612
  258.2 245.6 %all-reduce.13.cloned.1.call-start = ((), (), s32[]{:S(2)}) async-start(), calls=%async_computation.2 | async-start | bytes 524288 | tf_op jit(solution)/shard_map/psum | solution.py:9
  310.2 298.3 %all-reduce.15.cloned.1.call-start = ((), (), s32[]{:S(2)}) async-start(), calls=%async_computation.3 | async-start | bytes 1048576 | tf_op jit(solution)/shard_map/psum | solution.py:32
  553.7 0.8 copy-start.2
  558.4 245.4 %all-reduce.17.cloned.1.call-start = ((), (), s32[]{:S(2)}) async-start(), calls=%async_computation.4 | async-start | bytes 524288 | tf_op jit(solution)/shard_map/psum | solution.py:9
  610.5 300.0 %all-reduce.19.cloned.1.call-start = ((), (), s32[]{:S(2)}) async-start(), calls=%async_computation.5 | async-start | bytes 1048576 | tf_op jit(solution)/shard_map/psum | solution.py:32
  853.8 0.8 copy-start.3
  860.4 245.6 %all-reduce.21.cloned.1.call-start = ((), (), s32[]{:S(2)}) async-start(), calls=%async_computation.6 | async-start | bytes 524288 | tf_op jit(solution)/shard_map/psum | solution.py:9
  912.4 304.1 %all-reduce.23.cloned.1.call-start = ((), (), s32[]{:S(2)}) async-start(), calls=%async_computation.7 | async-start | bytes 2097152 | tf_op jit(solution)/shard_map/psum | solution.py:49
  1156.1 0.8 copy-start.4
Sparse Core Ops, SparseCore 0:
  11.8 193.6 all-reduce.8
  258.3 49.8 all-reduce.10
  312.0 191.7 all-reduce.12
  558.6 49.8 all-reduce.14
  612.1 191.7 all-reduce.16
  860.5 49.8 all-reduce.18
  914.2 191.7 all-reduce.20
  1163.2 53.3 all-reduce.22
where the time goes:
time: 1230 us
  waiting for transfers between devices  977 us (79%)
  blocking collectives  195 us (16%)
  other arithmetic  19 us (2%)
  between operations  15.6 us (1%)
    psum x4, waiting for transfers between devices, broadcast(): return lax.psum(jnp.where(mine, value, jnp.zeros_like(value)), axis)  775 us
    all_gather x4, blocking collectives, on_device(): sol = lax.all_gather(row_part, 'row', axis=0, tiled=True)  195 us
    psum x3, waiting for transfers between devices, on_device(): summed = lax.psum(pivot_part, 'col')  150 us
    psum x1, waiting for transfers between devices, on_device(): total = lax.psum(partial_value, 'col')  51.5 us
  transfers between devices with their start and end apart: 8, of which 8 were waited for; matrix products, arithmetic and copies ran while one was open for 0% of the time, Pallas kernels for 0%

commit v1 on v0

v1 whole, which is shorter than its diff:
```python
import functools

import jax
import jax.numpy as jnp
from jax import lax
from jax.experimental import pallas as pl
from jax.experimental.pallas import tpu as pltpu
from jax.sharding import PartitionSpec as P

MESH = pl.DeviceIdType.MESH
F32 = jnp.float32
BF16 = jnp.bfloat16
NY, NZ, NX = 8, 8, 4
BS, RHS = 1024, 128
PIECE = BS // 16


def remote(src, dst, ss, rs, row, col):
    return pltpu.make_async_remote_copy(
        src_ref=src, dst_ref=dst, send_sem=ss, recv_sem=rs,
        device_id={"row": row, "col": col}, device_id_type=MESH,
    )


def matmul(a_ref, b_ref, rows, store, tile=256):
    b = b_ref[...]
    if b.ndim == 3:
        b = b.reshape(BS, RHS)

    def body(i, carry):
        at = pl.ds(pl.multiple_of(i * tile, tile), tile)
        store(at, jnp.dot(a_ref[at, :], b, preferred_element_type=F32))
        return carry

    lax.fori_loop(0, rows // tile, body, 0)


def repack(src, dst, rows):
    def body(i, carry):
        part = src[pl.ds(i * 16, 16)].astype(F32).reshape(128, BS).astype(BF16)
        dst[pl.ds(pl.multiple_of(i * 128, 128), 128), :] = part
        return carry

    lax.fori_loop(0, rows // 128, body, 0)


def kernel(brow_ref, count_ref, rhs_hbm, diag_hbm, blk_hbm, solved_ref, rem_ref,
           rhs, blk, dq, dk, dm, acc, piv, qc, qn, qb, con, wts,
           loc, dsend, drecv, qsend, qrecv, p1send, prec, p2send, p3send, p3rec, p4send, p4rec,
           xsend, xrec, wsend, wrec):
    r = lax.axis_index("row")
    c = lax.axis_index("col")
    core = r % 2
    z = (r // 2) % NZ
    y = r // (2 * NZ)
    is_root = (c < 3) & (r == c + 1)
    support = ((c == 0) & ((r == 2) | (r == 3))) | ((c == 1) & (r == 3))
    early = is_root | support
    in_quarter = (r // 32) == c

    def at(yy, zz, kk):
        return (yy * NZ + zz) * 2 + kk

    barrier = pltpu.get_barrier_semaphore()

    def signal(row, col):
        pl.semaphore_signal(barrier, inc=1, device_id={"row": row, "col": col}, device_id_type=MESH)

    @pl.when(is_root)
    def _():
        def body(i, carry):
            signal((r + i) % 128, c)
            return carry

        lax.fori_loop(1, 128, body, 0)

    @pl.when(r == 0)
    def _():
        def body(i, carry):
            @pl.when((c > 0) | (i > 0))
            def _():
                signal(32 * c + i, c)
            return carry

        lax.fori_loop(0, 32, body, 0)

    @pl.when((c == 0) & (r >= 1) & (r <= 3))
    def _():
        for cc in range(4):
            signal(0, cc)

    @pl.when((c == 1) & (r == 2))
    def _():
        signal(1, 0)

    @pl.when((c == 2) & (r == 3))
    def _():
        signal(2, 1)

    @pl.when((c == 3) & (y == 0))
    def _():
        signal(3, 2)

    for d in range(1, 8):
        signal(at((y + d) % NY, z, core), c)
        signal(at(y, (z + d) % NZ, core), c)
        signal(at(y, (z + d) % NZ, 1 - core), c)
    signal(at(y, z, 1 - core), c)
    for d in range(1, 4):
        signal(r, (c + d) % NX)

    load_rhs = pltpu.make_async_copy(rhs_hbm, rhs, loc.at[0])
    load_blk = pltpu.make_async_copy(blk_hbm, blk, loc.at[1])
    load_rhs.start()
    load_blk.start()

    k_row = brow_ref[0]
    glob = k_row * 128 + r
    valid = (count_ref[0] > 0) & (glob > c)
    for i in range(2):
        w = jnp.where(valid & (k_row == i), F32(1.0), F32(0.0))
        wts[c, i] = jnp.full((8, RHS), w, F32)

    need = 25 + jnp.where((c < 3) & jnp.logical_not(is_root), 1, 0)
    need = need + jnp.where(in_quarter & (r > 0), 1, 0)
    need = need + jnp.where(r == 0, 3, 0)
    need = need + jnp.where((c < 2) & is_root, 1, 0)
    need = need + jnp.where((c == 2) & is_root, 16, 0)
    pl.semaphore_wait(barrier, need)

    @pl.when(in_quarter & (r > 0))
    def _():
        remote(diag_hbm.at[0], dq.at[r % 32], dsend.at[0], drecv.at[0], 0, c).start()

    @pl.when(in_quarter & (r == 0))
    def _():
        pltpu.make_async_copy(diag_hbm.at[0], dq.at[0], drecv.at[0]).start()

    @pl.when((c < 3) & jnp.logical_not(is_root))
    def _():
        remote(diag_hbm.at[c + 1], dk.at[r], dsend.at[1], drecv.at[1], c + 1, c).start()

    @pl.when(is_root)
    def _():
        pltpu.make_async_copy(diag_hbm.at[c + 1], dk.at[r], drecv.at[1]).start()

    for d in range(1, 4):
        remote(wts.at[c], wts.at[c], wsend.at[d - 1], wrec.at[c], r, (c + d) % NX).start()

    load_rhs.wait()
    load_blk.wait()

    def store_con(sl, v):
        con[c, sl, :] = v.astype(BF16)

    def send_con():
        for d in range(1, 4):
            remote(con.at[c], con.at[c], xsend.at[d - 1], xrec.at[c], r, (c + d) % NX).start()

    def wait_con(j):
        pltpu.make_async_copy(con.at[j], con.at[j], xrec.at[j]).wait()

    @pl.when(r == 0)
    def _():
        piv[...] = rhs[0].astype(BF16)
        pltpu.make_async_copy(dq, dq, drecv.at[0]).wait()
        repack(dq, dm, 256)

        def store(sl, v):
            qn[pl.ds(4 * c, 4)] = v.astype(BF16).reshape(4, PIECE, RHS)

        matmul(dm, piv, 256, store)
        for t in range(1, 4):
            part = pl.ds(4 * c, 4)
            remote(qn.at[part], qc.at[part], qsend.at[t - 1], qrecv, t, 0).start()

    @pl.when(is_root)
    def _():
        pltpu.make_async_copy(dk, dk, drecv.at[1]).wait()
        repack(dk, dm, BS)

    @pl.when(early)
    def _():
        pltpu.make_async_copy(qc, qc, qrecv).wait()

    @pl.when((c == 1) & (r == 2))
    def _():
        remote(qc, qc, qsend.at[1], qrecv, 3, 1).start()

    @pl.when(is_root)
    def _():
        def store(sl, v):
            acc[sl, :] = rhs[0, sl, :] - v
            con[c, sl, :] = v.astype(BF16)

        matmul(blk, qc, BS, store)

        def body(j, carry):
            wait_con(j)
            acc[...] = acc[...] - con[j].astype(F32)
            return carry

        lax.fori_loop(0, c, body, 0)
        piv[...] = acc[...].astype(BF16)

        def store_q(sl, v):
            n = v.shape[0] // PIECE
            qn[pl.ds(sl.start // PIECE, n)] = v.astype(BF16).reshape(n, PIECE, RHS)

        matmul(dm, piv, BS, store_q)

    @pl.when(is_root & (c < 2))
    def _():
        remote(qn, qc, qsend.at[0], qrecv, c + 2, c + 1).start()

    @pl.when(is_root & (c == 2))
    def _():
        for p in range(16):
            remote(qn.at[p], qb.at[p], p1send.at[p], prec, (p % 8) * 2 + p // 8, 3).start()

    @pl.when(is_root)
    def _():
        def body(p, carry):
            to = (p % 8) * 2 + p // 8

            @pl.when(to != r)
            def _():
                remote(qc.at[p], qb.at[p], p1send.at[16 + p], prec, to, c).start()

            @pl.when(to == r)
            def _():
                pltpu.make_async_copy(qc.at[p], qb.at[p], prec).start()

            return carry

        lax.fori_loop(0, 16, body, 0)

    @pl.when(support)
    def _():
        matmul(blk, qc, BS, store_con)

    @pl.when(early)
    def _():
        send_con()

    mine = core * 8 + z
    pltpu.make_async_copy(qb.at[mine], qb.at[mine], prec).wait()

    @pl.when(y == 0)
    def _():
        for d in (4, 3, 5, 2, 6, 1, 7):
            remote(qb.at[mine], qb.at[mine], p2send.at[d - 1], prec, at(d, z, core), c).start()

    for d in (4, 3, 5, 2, 6, 1, 7):
        remote(qb.at[mine], qb.at[mine], p3send.at[d - 1], p3rec, at(y, (z + d) % NZ, core), c).start()
    seven = qb.at[pl.ds(0, 7)]
    pltpu.make_async_copy(seven, seven, p3rec).wait()
    half = qb.at[pl.ds(8 * core, 8)]
    remote(half, half, p4send, p4rec, at(y, z, 1 - core), c).start()
    other = qb.at[pl.ds(8 * (1 - core), 8)]
    pltpu.make_async_copy(other, other, p4rec).wait()

    @pl.when(jnp.logical_not(early))
    def _():
        matmul(blk, qb, BS, store_con)
        send_con()

    solved_ref[...] = qb[...].astype(F32).reshape(BS, RHS)

    for j in range(4):
        @pl.when(c != j)
        def _():
            pltpu.make_async_copy(wts.at[j], wts.at[j], wrec.at[j]).wait()

            @pl.when(jnp.logical_not(is_root & (c > j)))
            def _():
                wait_con(j)

        base = rhs if j == 0 else rem_ref
        got = con[j].astype(F32).reshape(BS // 8, 8, RHS)
        for i in range(2):
            step = (got * wts[j, i][None]).reshape(BS, RHS)
            rem_ref[i] = base[i] - step

    @pl.when(in_quarter & (r > 0))
    def _():
        remote(diag_hbm.at[0], dq.at[0], dsend.at[0], drecv.at[0], 0, c).wait_send()

    @pl.when((c < 3) & jnp.logical_not(is_root))
    def _():
        remote(diag_hbm.at[0], dk.at[0], dsend.at[1], drecv.at[1], 0, c).wait_send()

    @pl.when(r == 0)
    def _():
        for t in range(3):
            part = pl.ds(0, 4)
            remote(qn.at[part], qc.at[part], qsend.at[t], qrecv, 1, 0).wait_send()

    @pl.when(is_root & (c < 2))
    def _():
        remote(qn, qc, qsend.at[0], qrecv, 0, 0).wait_send()

    @pl.when((c == 1) & (r == 2))
    def _():
        remote(qc, qc, qsend.at[1], qrecv, 0, 0).wait_send()

    @pl.when(is_root & (c == 2))
    def _():
        for p in range(16):
            remote(qn.at[0], qb.at[0], p1send.at[p], prec, 0, 3).wait_send()

    @pl.when(is_root)
    def _():
        def body(p, carry):
            @pl.when((p % 8) * 2 + p // 8 != r)
            def _():
                remote(qc.at[0], qb.at[0], p1send.at[16 + p], prec, 0, c).wait_send()
            return carry

        lax.fori_loop(0, 16, body, 0)

    @pl.when(y == 0)
    def _():
        for d in range(7):
            remote(qb.at[0], qb.at[0], p2send.at[d], prec, 0, c).wait_send()

    for d in range(7):
        remote(qb.at[0], qb.at[0], p3send.at[d], p3rec, 0, c).wait_send()
    remote(half, half, p4send, p4rec, 0, c).wait_send()
    for d in range(3):
        remote(con.at[0], con.at[0], xsend.at[d], xrec.at[0], 0, c).wait_send()
        remote(wts.at[0], wts.at[0], wsend.at[d], wrec.at[0], 0, c).wait_send()


def on_device(rhs, diag_inv, blocks, block_rows, counts):
    vmem = pl.BlockSpec(memory_space=pltpu.VMEM)
    smem = pl.BlockSpec(memory_space=pltpu.SMEM)
    hbm = pl.BlockSpec(memory_space=pl.ANY)
    dma = pltpu.SemaphoreType.DMA
    solved, rem = pl.pallas_call(
        kernel,
        out_shape=(
            jax.ShapeDtypeStruct((BS, RHS), F32),
            jax.ShapeDtypeStruct((2, BS, RHS), F32),
        ),
        in_specs=[smem, smem, hbm, hbm, hbm],
        out_specs=(vmem, vmem),
        scratch_shapes=[
            pltpu.VMEM((2, BS, RHS), F32),
            pltpu.VMEM((BS, BS), BF16),
            pltpu.VMEM((32, 8, BS), BF16),
            pltpu.VMEM((128, 8, BS), BF16),
            pltpu.VMEM((BS, BS), BF16),
            pltpu.VMEM((BS, RHS), F32),
            pltpu.VMEM((BS, RHS), BF16),
            pltpu.VMEM((16, PIECE, RHS), BF16),
            pltpu.VMEM((16, PIECE, RHS), BF16),
            pltpu.VMEM((16, PIECE, RHS), BF16),
            pltpu.VMEM((4, BS, RHS), BF16),
            pltpu.VMEM((4, 2, 8, RHS), F32),
            dma((2,)), dma((2,)), dma((2,)), dma((3,)), dma,
            dma((32,)), dma, dma((7,)), dma((7,)), dma, dma, dma,
            dma((3,)), dma((4,)), dma((3,)), dma((4,)),
        ],
        compiler_params=pltpu.CompilerParams(
            collective_id=0, has_side_effects=True, vmem_limit_bytes=40 << 20
        ),
    )(
        block_rows.reshape(1), counts.reshape(1), rhs.reshape(2, BS, RHS), diag_inv,
        blocks.reshape(BS, BS),
    )
    return solved.reshape(1, 1, BS, RHS), rem.reshape(2, 1, BS, RHS)


def solution(mesh):
    in_specs = (
        P(None, "row", None, None),
        P(None, "row", None),
        P(None, "col", "row", None, None, None),
        P(None, "col", "row", None),
        P(None, "col", "row"),
    )
    out_specs = (P(None, "col", None, None), P(None, "row", None, None))
    return jax.shard_map(
        on_device, mesh=mesh, in_specs=in_specs, out_specs=out_specs, check_vma=False
    )
```

time: 1230 us -> 97.2 us (0.08)
  waiting for transfers between devices: 977 us -> 0 us
  blocking collectives: 195 us -> 0 us
  Pallas kernels: 0 us -> 89.6 us
  other arithmetic: 19 us -> 0 us
  between operations: 15.6 us -> 1.94 us
    psum x8 -> x0, waiting for transfers between devices: 977 us -> none  [the longest x4 775 us: broadcast(): return lax.psum(jnp.where(mine, value, jnp.zeros_like(value)), axis)]
    all_gather x4 -> x0, blocking collectives: 195 us -> none  [on_device(): sol = lax.all_gather(row_part, 'row', axis=0, tiled=True)]
    pallas_call x0 -> x1, Pallas kernels: none -> 89.6 us  [on_device(): pl.pallas_call(kernel, out_shape=(jax.ShapeDtypeStruct((BS, RHS), F32), j...]
  transfers between devices with their start and end apart: 8 -> 0, of which waited for: 8 -> 0; matrix products, arithmetic and copies ran while one was open for 0% -> 0% of each run, Pallas kernels for 0% -> 0%
where the time goes in v1:
time: 97.2 us; the launch traced here: 97 us
  Pallas kernels  89.6 us (92%)
  local copies, waits for them, and re-layouts  5.41 us (6%)
  between operations  1.94 us (2%)
    pallas_call x1, Pallas kernels, on_device(): pl.pallas_call(kernel, out_shape=(jax.ShapeDtypeStruct((BS, RHS), F32), j...  89.6 us
    unnamed x8, local copies, waits for them, and re-layouts  5.41 us

profile of v1, /device:TPU:9, one launch (start us, length us, event | category | flops | bytes accessed | tf_op | source)
XLA Modules:
  0.0 97.0 jit_solution(10591484335533442783)
XLA Ops:
  1.9 0.0 copy-start
  1.9 1.6 %copy-done = bf16[1,1,1,1,1024,1024]{5,4,3,2,1,0:T(8,128)(2,1)S(1)} copy-done((bf16[1,1,1,1,1024,1024]{5,4,3,2,1,0:T(8,128)(2,1)S(1)}, bf16[1,1,1,1,1024,1024]{5,4,3,2,1,0:T(8,128)(2,1)}, u32[]{:S(2)}) %copy-start) | copy-done | bytes 2097176
  3.5 0.0 copy-start.1
  3.5 1.2 %copy-done.1 = f32[2,1,1024,128]{3,2,1,0:T(8,128)S(1)} copy-done((f32[2,1,1024,128]{3,2,1,0:T(8,128)S(1)}, f32[2,1,1024,128]{3,2,1,0:T(8,128)}, u32[]{:S(2)}) %copy-start.1) | copy-done | bytes 1048600
  4.7 0.0 copy-start.2
  4.7 0.8 copy-done.2
  5.6 89.6 %shard_map.68 = (f32[1024,128]{1,0:T(8,128)S(1)}, f32[2,1024,128]{2,1,0:T(8,128)S(1)}) custom-call(s32[1]{0:T(128)} %bitcast.8.brow_ref, s32[1]{0:T(128)} %bitcast.9.count_ref, f32[2,1024,128]{2,1,0:T(8,128)S(1)} %bitcast.11, bf16[4,8,1024]{2,1,0:T(8,128)(2,1)S(1)} %copy-done.2, bf16[1024,1024]{1,0:T(8,128)(2,1)S(1)} %bitcast.10), custom_call_target="tpu_custom_call" | custom-call | tf_op jit(solution)/shard_map/pallas_call | solution.py:340
  95.2 0.8 copy.12
  96.0 1.0 copy.13
Async XLA Ops:
  1.9 1.6 %copy-start = (bf16[1,1,1,1,1024,1024]{5,4,3,2,1,0:T(8,128)(2,1)S(1)}, bf16[1,1,1,1,1024,1024]{5,4,3,2,1,0:T(8,128)(2,1)}, u32[]{:S(2)}) copy-start(bf16[1,1,1,1,1024,1024]{5,4,3,2,1,0:T(8,128)(2,1)} %param.7) | copy-start | bytes 6291460
  3.5 1.2 %copy-start.1 = (f32[2,1,1024,128]{3,2,1,0:T(8,128)S(1)}, f32[2,1,1024,128]{3,2,1,0:T(8,128)}, u32[]{:S(2)}) copy-start(f32[2,1,1024,128]{3,2,1,0:T(8,128)} %param.5) | copy-start | bytes 3145732
  4.7 0.8 copy-start.2

commit v2 on v1

v2 whole, which is shorter than its diff:
```python
import functools

import jax
import jax.numpy as jnp
from jax import lax
from jax.experimental import pallas as pl
from jax.experimental.pallas import tpu as pltpu
from jax.sharding import PartitionSpec as P

MESH = pl.DeviceIdType.MESH
F32 = jnp.float32
BF16 = jnp.bfloat16
NY, NZ, NX = 8, 8, 4
BS, RHS = 1024, 128
PIECE = BS // 16


def remote(src, dst, ss, rs, row, col):
    return pltpu.make_async_remote_copy(
        src_ref=src, dst_ref=dst, send_sem=ss, recv_sem=rs,
        device_id={"row": row, "col": col}, device_id_type=MESH,
    )


def kernel(brow_ref, count_ref, rhs_hbm, diag_hbm, blk_hbm, solved_ref, rem_ref,
           rhs, blk, dq, dk, dm, own, rhs_left, piv, qc, qn, qb, con, wts,
           loc, dsend, d0rec, drec, qsend, qrec, fsend, p1send, prec, p2send, p3send, p3rec, p4send, p4rec,
           xsend, xrec, x3send, x3rec, wsend, wrec):
    r = lax.axis_index("row")
    c = lax.axis_index("col")
    core = r % 2
    z = (r // 2) % NZ
    y = r // (2 * NZ)
    is_root = (c < 3) & (r == c + 1)
    support = ((c == 0) & ((r == 2) | (r == 3))) | ((c == 1) & (r == 3))
    early = is_root | support
    in_quarter = (r // 32) == c

    def at(yy, zz, kk):
        return (yy * NZ + zz) * 2 + kk

    drains = []

    def later(cond, *copies):
        def go():
            for copy in copies:
                copy.wait_send()

        drains.append(go if cond is None else lambda: pl.when(cond)(go))

    def finish():
        for drain in drains:
            drain()

    barrier = pltpu.get_barrier_semaphore()

    def signal(row, col):
        pl.semaphore_signal(barrier, inc=1, device_id={"row": row, "col": col}, device_id_type=MESH)

    @pl.when(is_root)
    def _():
        def body(i, carry):
            signal((r + i) % 128, c)
            return carry

        lax.fori_loop(1, 128, body, 0)

    @pl.when(r == 0)
    def _():
        def body(i, carry):
            @pl.when((c > 0) | (i > 0))
            def _():
                signal(32 * c + i, c)
            return carry

        lax.fori_loop(0, 32, body, 0)

    @pl.when((c == 0) & (r >= 1) & (r <= 3))
    def _():
        for cc in range(4):
            signal(0, cc)

    @pl.when((c == 1) & (r == 2))
    def _():
        signal(1, 0)

    @pl.when((c == 2) & (r == 3))
    def _():
        signal(2, 1)

    @pl.when((c == 3) & (y == 0))
    def _():
        signal(3, 2)

    for d in range(1, 8):
        signal(at((y + d) % NY, z, core), c)
        signal(at(y, (z + d) % NZ, core), c)
        signal(at(y, (z + d) % NZ, 1 - core), c)
    signal(at(y, z, 1 - core), c)
    for d in range(1, 4):
        signal(r, (c + d) % NX)

    load_rhs = pltpu.make_async_copy(rhs_hbm, rhs, loc.at[0])
    load_blk = pltpu.make_async_copy(blk_hbm, blk, loc.at[1])
    load_rhs.start()
    load_blk.start()

    k_row = brow_ref[0]
    glob = k_row * 128 + r
    valid = (count_ref[0] > 0) & (glob > c)
    for i in range(2):
        w = jnp.where(valid & (k_row == i), F32(1.0), F32(0.0))
        wts[c, i] = jnp.full((8, RHS), w, F32)

    need = 25 + jnp.where((c < 3) & jnp.logical_not(is_root), 1, 0)
    need = need + jnp.where(in_quarter & (r > 0), 1, 0)
    need = need + jnp.where(r == 0, 3, 0)
    need = need + jnp.where((c < 2) & is_root, 1, 0)
    need = need + jnp.where((c == 2) & is_root, 16, 0)
    pl.semaphore_wait(barrier, need)

    for yy in range(NY):
        width = pl.ds(0, 128 * (yy + 1))

        @pl.when((y == yy) & in_quarter)
        def _():
            @pl.when(r > 0)
            def _():
                remote(diag_hbm.at[0, :, width], dq.at[r % 32, :, width], dsend.at[0], d0rec.at[yy % 2], 0, c).start()

            @pl.when(r == 0)
            def _():
                pltpu.make_async_copy(diag_hbm.at[0, :, width], dq.at[r % 32, :, width], d0rec.at[yy % 2]).start()

        @pl.when((y == yy) & (c < 3))
        def _():
            @pl.when(jnp.logical_not(is_root))
            def _():
                remote(diag_hbm.at[c + 1, :, width], dk.at[r, :, width], dsend.at[1], drec.at[yy], c + 1, c).start()

            @pl.when(is_root)
            def _():
                pltpu.make_async_copy(diag_hbm.at[c + 1, :, width], dk.at[r, :, width], drec.at[yy]).start()

        later((y == yy) & in_quarter & (r > 0),
              remote(diag_hbm.at[0, :, width], dq.at[0, :, width], dsend.at[0], d0rec.at[0], 0, c))
        later((y == yy) & (c < 3) & jnp.logical_not(is_root),
              remote(diag_hbm.at[0, :, width], dk.at[0, :, width], dsend.at[1], drec.at[0], 0, c))

    for d in range(1, 4):
        remote(wts.at[c], wts.at[c], wsend.at[d - 1], wrec.at[c], r, (c + d) % NX).start()

    load_rhs.wait()
    load_blk.wait()

    for d in range(3):
        later(None, remote(wts.at[0], wts.at[0], wsend.at[d], wrec.at[0], 0, c))

    def send_con(d):
        remote(con.at[c], con.at[c], xsend.at[d - 1], xrec.at[c], r, (c + d) % NX).start()

    def wait_con(j):
        pltpu.make_async_copy(con.at[j], con.at[j], xrec.at[j]).wait()

    def squeeze(ref, block, width):
        part = ref[pl.ds(16 * block, 16), :, pl.ds(0, width)]
        return part.astype(F32).reshape(128, width).astype(BF16)

    def put_q(block, v):
        qn[pl.ds(2 * block, 2)] = v.astype(BF16).reshape(2, PIECE, RHS)

    for cc in range(NX):
        @pl.when((r == 0) & (c == cc))
        def _():
            piv[...] = rhs[0].astype(BF16)
            for h in range(2):
                block = 2 * cc + h
                width = 128 * (block + 1)
                sixteen = dq.at[pl.ds(16 * h, 16), :, pl.ds(0, width)]
                pltpu.make_async_copy(sixteen, sixteen, d0rec.at[h]).wait()
                put_q(block, jnp.dot(squeeze(dq, h, width), piv[pl.ds(0, width), :], preferred_element_type=F32))
            part = pl.ds(4 * cc, 4)
            for t in range(1, 4):
                remote(qn.at[part], qc.at[part], qsend.at[t - 1], qrec.at[cc], t, 0).start()

    part0 = pl.ds(0, 4)
    later(r == 0, *[remote(qn.at[part0], qc.at[part0], qsend.at[t], qrec.at[0], 1, 0) for t in range(3)])

    @pl.when(is_root)
    def _():
        for block in range(8):
            width = 128 * (block + 1)
            sixteen = dk.at[pl.ds(16 * block, 16), :, pl.ds(0, width)]
            pltpu.make_async_copy(sixteen, sixteen, drec.at[block]).wait()
            dm[pl.ds(128 * block, 128), pl.ds(0, width)] = squeeze(dk, block, width)

    @pl.when(early)
    def _():
        for g in range(4):
            part = pl.ds(4 * g, 4)
            pltpu.make_async_copy(qc.at[part], qc.at[part], qrec.at[g]).wait()

            @pl.when((c == 1) & (r == 2))
            def _():
                remote(qc.at[part], qc.at[part], fsend.at[g], qrec.at[g], 3, 1).start()

            b = qc[part].reshape(256, RHS)

            def body(i, carry):
                at_rows = pl.ds(pl.multiple_of(i * 256, 256), 256)
                step = jnp.dot(blk[at_rows, pl.ds(256 * g, 256)], b, preferred_element_type=F32)
                own[at_rows, :] = step if g == 0 else own[at_rows, :] + step
                return carry

            lax.fori_loop(0, 4, body, 0)

    @pl.when(is_root)
    def _():
        def body(j, carry):
            wait_con(j)
            rhs_left[...] = rhs_left[...] - con[j].astype(F32)
            return carry

        rhs_left[...] = rhs[0]
        lax.fori_loop(0, c, body, 0)
        piv[...] = (rhs_left[...] - own[...]).astype(BF16)
        for block in range(8):
            width = 128 * (block + 1)
            put_q(block, jnp.dot(dm[pl.ds(128 * block, 128), pl.ds(0, width)], piv[pl.ds(0, width), :],
                                 preferred_element_type=F32))

            @pl.when(c == 2)
            def _():
                for p in (2 * block, 2 * block + 1):
                    remote(qn.at[p], qb.at[p], p1send.at[p], prec, (p % 8) * 2 + p // 8, 3).start()

            if block % 2 == 1:
                @pl.when(c < 2)
                def _():
                    part = pl.ds(2 * block - 2, 4)
                    remote(qn.at[part], qc.at[part], qsend.at[block // 2], qrec.at[block // 2], c + 2, c + 1).start()

    later((c == 1) & (r == 2), *[remote(qc.at[part0], qc.at[part0], fsend.at[g], qrec.at[0], 0, 0) for g in range(4)])
    later(is_root & (c < 2), *[remote(qn.at[part0], qc.at[part0], qsend.at[g], qrec.at[0], 0, 0) for g in range(4)])
    later(is_root & (c == 2), *[remote(qn.at[0], qb.at[0], p1send.at[p], prec, 0, 3) for p in range(16)])

    @pl.when(early)
    def _():
        con[c] = own[...].astype(BF16)

    for d in (1, 2):
        @pl.when(support & (c + d == r - 1))
        def _():
            send_con(d)

    @pl.when(is_root)
    def _():
        def body(p, carry):
            to = (p % 8) * 2 + p // 8

            @pl.when(to != r)
            def _():
                remote(qc.at[p], qb.at[p], p1send.at[16 + p], prec, to, c).start()

            @pl.when(to == r)
            def _():
                pltpu.make_async_copy(qc.at[p], qb.at[p], prec).start()

            return carry

        lax.fori_loop(0, 16, body, 0)

    for p in range(16):
        later(is_root & ((p % 8) * 2 + p // 8 != r), remote(qc.at[0], qb.at[0], p1send.at[16 + p], prec, 0, c))

    mine = core * 8 + z
    pltpu.make_async_copy(qb.at[mine], qb.at[mine], prec).wait()


    @pl.when(y == 0)
    def _():
        for d in (4, 3, 5, 2, 6, 1, 7):
            remote(qb.at[mine], qb.at[mine], p2send.at[d - 1], prec, at(d, z, core), c).start()

    later(y == 0, *[remote(qb.at[0], qb.at[0], p2send.at[d], prec, 0, c) for d in range(7)])
    for d in (4, 3, 5, 2, 6, 1, 7):
        remote(qb.at[mine], qb.at[mine], p3send.at[d - 1], p3rec, at(y, (z + d) % NZ, core), c).start()
    seven = qb.at[pl.ds(0, 7)]
    pltpu.make_async_copy(seven, seven, p3rec).wait()
    later(None, *[remote(qb.at[0], qb.at[0], p3send.at[d], p3rec, 0, c) for d in range(7)])
    half = qb.at[pl.ds(8 * core, 8)]
    remote(half, half, p4send, p4rec, at(y, z, 1 - core), c).start()
    other = qb.at[pl.ds(8 * (1 - core), 8)]
    pltpu.make_async_copy(other, other, p4rec).wait()
    later(None, remote(half, half, p4send, p4rec, 0, c))

    def quarter(j, t):
        return con.at[j, pl.ds(256 * t, 256)]

    def send_quarter(t, col, slot):
        remote(quarter(3, t), quarter(3, t), x3send.at[slot], x3rec.at[t], r, col).start()

    def compute(t):
        at_rows = pl.ds(256 * t, 256)
        b = qb[...].reshape(BS, RHS)
        con[c, at_rows, :] = jnp.dot(blk[at_rows, :], b, preferred_element_type=F32).astype(BF16)

    @pl.when(c == 3)
    def _():
        for t, col in ((0, 0), (2, 2), (1, 0), (3, 2)):
            compute(t)
            send_quarter(t, col, t)
        for t, col in ((2, 0), (0, 2), (3, 0), (1, 2)):
            send_quarter(t, col, 4 + t)

    @pl.when((c < 3) & jnp.logical_not(early))
    def _():
        for t in range(4):
            compute(t)

    for d in (1, 3, 2):
        @pl.when((c < 3) & jnp.logical_not(support & (c + d == r - 1)))
        def _():
            send_con(d)

    later(c < 3, *[remote(con.at[0], con.at[0], xsend.at[d], xrec.at[0], 0, c) for d in range(3)])
    later(c == 3, *[remote(quarter(3, 0), quarter(3, 0), x3send.at[t], x3rec.at[0], 0, c) for t in range(8)])
    later((c == 0) | (c == 2), *[remote(quarter(3, 0), quarter(3, 0), x3send.at[t], x3rec.at[0], 0, c) for t in range(2)])

    solved_ref[...] = qb[...].astype(F32).reshape(BS, RHS)

    for j in range(4):
        @pl.when(c != j)
        def _():
            pltpu.make_async_copy(wts.at[j], wts.at[j], wrec.at[j]).wait()

    def update(j, base, rows):
        got = con[j, rows, :].astype(F32).reshape(rows.size // 8, 8, RHS)
        for i in range(2):
            step = (got * wts[j, i][None]).reshape(rows.size, RHS)
            rem_ref[i, rows, :] = base[i, rows, :] - step

    for j in range(3):
        @pl.when((c != j) & jnp.logical_not(is_root & (c > j)))
        def _():
            wait_con(j)

        update(j, rhs if j == 0 else rem_ref, pl.ds(0, BS))

    for t in (0, 1, 2, 3):
        @pl.when(c == 0)
        def _():
            pltpu.make_async_copy(quarter(3, t), quarter(3, t), x3rec.at[t]).wait()
            if t < 2:
                send_quarter(t, 1, t)

        u = (t + 2) % 4

        @pl.when(c == 2)
        def _():
            pltpu.make_async_copy(quarter(3, u), quarter(3, u), x3rec.at[u]).wait()
            if u >= 2:
                send_quarter(u, 1, u - 2)

        @pl.when(c == 1)
        def _():
            v = (0, 2, 1, 3)[t]
            pltpu.make_async_copy(quarter(3, v), quarter(3, v), x3rec.at[v]).wait()

    update(3, rem_ref, pl.ds(0, BS))

    finish()


def on_device(rhs, diag_inv, blocks, block_rows, counts):
    vmem = pl.BlockSpec(memory_space=pltpu.VMEM)
    smem = pl.BlockSpec(memory_space=pltpu.SMEM)
    hbm = pl.BlockSpec(memory_space=pltpu.HBM)
    dma = pltpu.SemaphoreType.DMA
    solved, rem = pl.pallas_call(
        kernel,
        out_shape=(
            jax.ShapeDtypeStruct((BS, RHS), F32),
            jax.ShapeDtypeStruct((2, BS, RHS), F32),
        ),
        in_specs=[smem, smem, hbm, hbm, hbm],
        out_specs=(vmem, vmem),
        scratch_shapes=[
            pltpu.VMEM((2, BS, RHS), F32),
            pltpu.VMEM((BS, BS), BF16),
            pltpu.VMEM((32, 8, BS), BF16),
            pltpu.VMEM((128, 8, BS), BF16),
            pltpu.VMEM((BS, BS), BF16),
            pltpu.VMEM((BS, RHS), F32),
            pltpu.VMEM((BS, RHS), F32),
            pltpu.VMEM((BS, RHS), BF16),
            pltpu.VMEM((16, PIECE, RHS), BF16),
            pltpu.VMEM((16, PIECE, RHS), BF16),
            pltpu.VMEM((16, PIECE, RHS), BF16),
            pltpu.VMEM((4, BS, RHS), BF16),
            pltpu.VMEM((4, 2, 8, RHS), F32),
            dma((2,)), dma((2,)), dma((2,)), dma((8,)), dma((4,)), dma((4,)), dma((4,)),
            dma((32,)), dma, dma((7,)), dma((7,)), dma, dma, dma,
            dma((3,)), dma((3,)), dma((8,)), dma((4,)), dma((3,)), dma((4,)),
        ],
        compiler_params=pltpu.CompilerParams(
            collective_id=0, has_side_effects=True, vmem_limit_bytes=40 << 20
        ),
    )(
        block_rows.reshape(1), counts.reshape(1), rhs.reshape(2, BS, RHS), diag_inv,
        blocks.reshape(BS, BS),
    )
    return solved.reshape(1, 1, BS, RHS), rem.reshape(2, 1, BS, RHS)


def solution(mesh):
    in_specs = (
        P(None, "row", None, None),
        P(None, "row", None),
        P(None, "col", "row", None, None, None),
        P(None, "col", "row", None),
        P(None, "col", "row"),
    )
    out_specs = (P(None, "col", None, None), P(None, "row", None, None))
    return jax.shard_map(
        on_device, mesh=mesh, in_specs=in_specs, out_specs=out_specs, check_vma=False
    )
```

time: 97.2 us -> 91 us (0.936)
  the two profiles are of different devices: /device:TPU:9 before, /device:TPU:11 now
where the time goes in v2:
time: 91 us; the launch traced here: 90.7 us
  Pallas kernels  83.4 us (92%)
  local copies, waits for them, and re-layouts  5.41 us (6%)
  between operations  1.94 us (2%)
    pallas_call x1, Pallas kernels, on_device(): pl.pallas_call(kernel, out_shape=(jax.ShapeDtypeStruct((BS, RHS), F32), j...  83.4 us
    unnamed x8, local copies, waits for them, and re-layouts  5.41 us

profile of v2, /device:TPU:11, one launch (start us, length us, event | category | flops | bytes accessed | tf_op | source)
XLA Modules:
  0.0 90.7 jit_solution(10567775751766735561)
XLA Ops:
  1.9 0.0 copy-start
  1.9 1.6 %copy-done = bf16[1,1,1,1,1024,1024]{5,4,3,2,1,0:T(8,128)(2,1)S(1)} copy-done((bf16[1,1,1,1,1024,1024]{5,4,3,2,1,0:T(8,128)(2,1)S(1)}, bf16[1,1,1,1,1024,1024]{5,4,3,2,1,0:T(8,128)(2,1)}, u32[]{:S(2)}) %copy-start) | copy-done | bytes 2097176
  3.5 0.0 copy-start.1
  3.5 1.2 %copy-done.1 = f32[2,1,1024,128]{3,2,1,0:T(8,128)S(1)} copy-done((f32[2,1,1024,128]{3,2,1,0:T(8,128)S(1)}, f32[2,1,1024,128]{3,2,1,0:T(8,128)}, u32[]{:S(2)}) %copy-start.1) | copy-done | bytes 1048600
  4.7 0.0 copy-start.2
  4.7 0.8 copy-done.2
  5.6 83.4 %shard_map.68 = (f32[1024,128]{1,0:T(8,128)S(1)}, f32[2,1024,128]{2,1,0:T(8,128)S(1)}) custom-call(s32[1]{0:T(128)} %bitcast.8.brow_ref, s32[1]{0:T(128)} %bitcast.9.count_ref, f32[2,1024,128]{2,1,0:T(8,128)S(1)} %bitcast.11, bf16[4,8,1024]{2,1,0:T(8,128)(2,1)S(1)} %copy-done.2, bf16[1024,1024]{1,0:T(8,128)(2,1)S(1)} %bitcast.10), custom_call_target="tpu_custom_call" | custom-call | tf_op jit(solution)/shard_map/pallas_call | solution.py:380
  89.0 0.8 copy.12
  89.8 1.0 %copy.13 = f32[2,1,1024,128]{3,2,1,0:T(8,128)} copy(f32[2,1,1024,128]{3,2,1,0:T(8,128)S(1)} %bitcast.12) | data formatting | bytes 2097152
Async XLA Ops:
  1.9 1.6 %copy-start = (bf16[1,1,1,1,1024,1024]{5,4,3,2,1,0:T(8,128)(2,1)S(1)}, bf16[1,1,1,1,1024,1024]{5,4,3,2,1,0:T(8,128)(2,1)}, u32[]{:S(2)}) copy-start(bf16[1,1,1,1,1024,1024]{5,4,3,2,1,0:T(8,128)(2,1)} %param.7) | copy-start | bytes 6291460
  3.5 1.2 %copy-start.1 = (f32[2,1,1024,128]{3,2,1,0:T(8,128)S(1)}, f32[2,1,1024,128]{3,2,1,0:T(8,128)}, u32[]{:S(2)}) copy-start(f32[2,1,1024,128]{3,2,1,0:T(8,128)} %param.5) | copy-start | bytes 3145732
  4.7 0.8 copy-start.2

commit v3 on v2

--- a/solution.py
+++ b/solution.py
@@ -23,9 +23,9 @@
 
 
 def kernel(brow_ref, count_ref, rhs_hbm, diag_hbm, blk_hbm, solved_ref, rem_ref,
-           rhs, blk, dq, dk, dm, own, rhs_left, piv, qc, qn, qb, con, wts,
+           rhs, blk, blk2, dq, dk, dm, own, rhs_left, piv, qc, qn, qb, con, wts,
            loc, dsend, d0rec, drec, qsend, qrec, fsend, p1send, prec, p2send, p3send, p3rec, p4send, p4rec,
-           xsend, xrec, x3send, x3rec, wsend, wrec):
+           xsend, xrec, hsend, hrec, wsend, wrec, bsend, brec):
     r = lax.axis_index("row")
     c = lax.axis_index("col")
     core = r % 2
@@ -75,22 +75,26 @@
 
         lax.fori_loop(0, 32, body, 0)
 
-    @pl.when((c == 0) & (r >= 1) & (r <= 3))
-    def _():
-        for cc in range(4):
-            signal(0, cc)
-
-    @pl.when((c == 1) & (r == 2))
-    def _():
-        signal(1, 0)
-
-    @pl.when((c == 2) & (r == 3))
-    def _():
-        signal(2, 1)
-
-    @pl.when((c == 3) & (y == 0))
-    def _():
-        signal(3, 2)
+    @pl.when(y == 0)
+    def _():
+        @pl.when(c == 0)
+        def _():
+            for cc in range(NX):
+                @pl.when((r > 0) | (cc > 0))
+                def _():
+                    signal(0, cc)
+
+        @pl.when(c == 1)
+        def _():
+            signal(1, 0)
+
+        @pl.when(c == 2)
+        def _():
+            signal(2, 1)
+
+        @pl.when(c % 2 == 1)
+        def _():
+            signal(3, 2)
 
     for d in range(1, 8):
         signal(at((y + d) % NY, z, core), c)
@@ -114,9 +118,8 @@
 
     need = 25 + jnp.where((c < 3) & jnp.logical_not(is_root), 1, 0)
     need = need + jnp.where(in_quarter & (r > 0), 1, 0)
-    need = need + jnp.where(r == 0, 3, 0)
-    need = need + jnp.where((c < 2) & is_root, 1, 0)
-    need = need + jnp.where((c == 2) & is_root, 16, 0)
+    need = need + jnp.where(r == 0, jnp.where(c == 0, 15, 16), 0)
+    need = need + jnp.where(is_root, jnp.where(c == 2, 32, 16), 0)
     pl.semaphore_wait(barrier, need)
 
     for yy in range(NY):
@@ -147,6 +150,14 @@
         later((y == yy) & (c < 3) & jnp.logical_not(is_root),
               remote(diag_hbm.at[0, :, width], dk.at[0, :, width], dsend.at[1], drec.at[0], 0, c))
 
+    pair = (c == 3) & (r >= 4)
+
+    @pl.when(pair)
+    def _():
+        remote(blk_hbm, blk2, bsend, brec, r, 1).start()
+
+    later(pair, remote(blk_hbm, blk2, bsend, brec, r, 0))
+
     for d in range(1, 4):
         remote(wts.at[c], wts.at[c], wsend.at[d - 1], wrec.at[c], r, (c + d) % NX).start()
 
@@ -161,6 +172,9 @@
 
     def wait_con(j):
         pltpu.make_async_copy(con.at[j], con.at[j], xrec.at[j]).wait()
+
+    def line(p):
+        return (p % NZ) * 2 + p // NZ
 
     def squeeze(ref, block, width):
         part = ref[pl.ds(16 * block, 16), :, pl.ds(0, width)]
@@ -182,7 +196,14 @@
             part = pl.ds(4 * cc, 4)
             for t in range(1, 4):
                 remote(qn.at[part], qc.at[part], qsend.at[t - 1], qrec.at[cc], t, 0).start()
-
+            for p in range(4 * cc, 4 * cc + 4):
+                if p == 0:
+                    pltpu.make_async_copy(qn.at[p], qb.at[0, p], prec.at[0]).start()
+                else:
+                    remote(qn.at[p], qb.at[0, p], p1send.at[0, p % 4], prec.at[0], line(p), 0).start()
+
+    for p in range(4):
+        later((r == 0) & ((c > 0) | (p > 0)), remote(qn.at[p], qb.at[0, p], p1send.at[0, p], prec.at[0], 0, 0))
     part0 = pl.ds(0, 4)
     later(r == 0, *[remote(qn.at[part0], qc.at[part0], qsend.at[t], qrec.at[0], 1, 0) for t in range(3)])
 
@@ -213,6 +234,15 @@
                 return carry
 
             lax.fori_loop(0, 4, body, 0)
+
+    def scatter(p):
+        k = c + 1
+        slot = k // 2
+        remote(qn.at[p], qb.at[slot, p], p1send.at[0, p], prec.at[slot], line(p), k).start()
+
+        @pl.when(c == 2)
+        def _():
+            remote(qn.at[p], qb.at[slot, p], p1send.at[1, p], prec.at[slot], line(p), 1).start()
 
     @pl.when(is_root)
     def _():
@@ -232,7 +262,7 @@
             @pl.when(c == 2)
             def _():
                 for p in (2 * block, 2 * block + 1):
-                    remote(qn.at[p], qb.at[p], p1send.at[p], prec, (p % 8) * 2 + p // 8, 3).start()
+                    scatter(p)
 
             if block % 2 == 1:
                 @pl.when(c < 2)
@@ -242,7 +272,9 @@
 
     later((c == 1) & (r == 2), *[remote(qc.at[part0], qc.at[part0], fsend.at[g], qrec.at[0], 0, 0) for g in range(4)])
     later(is_root & (c < 2), *[remote(qn.at[part0], qc.at[part0], qsend.at[g], qrec.at[0], 0, 0) for g in range(4)])
-    later(is_root & (c == 2), *[remote(qn.at[0], qb.at[0], p1send.at[p], prec, 0, 3) for p in range(16)])
+    for p in range(16):
+        later(is_root, remote(qn.at[p], qb.at[0, p], p1send.at[0, p], prec.at[0], 0, 3))
+        later(is_root & (c == 2), remote(qn.at[p], qb.at[0, p], p1send.at[1, p], prec.at[0], 0, 3))
 
     @pl.when(early)
     def _():
@@ -253,81 +285,108 @@
         def _():
             send_con(d)
 
-    @pl.when(is_root)
-    def _():
-        def body(p, carry):
-            to = (p % 8) * 2 + p // 8
-
-            @pl.when(to != r)
-            def _():
-                remote(qc.at[p], qb.at[p], p1send.at[16 + p], prec, to, c).start()
-
-            @pl.when(to == r)
-            def _():
-                pltpu.make_async_copy(qc.at[p], qb.at[p], prec).start()
-
-            return carry
-
-        lax.fori_loop(0, 16, body, 0)
-
-    for p in range(16):
-        later(is_root & ((p % 8) * 2 + p // 8 != r), remote(qc.at[0], qb.at[0], p1send.at[16 + p], prec, 0, c))
+    @pl.when(is_root & (c < 2))
+    def _():
+        for p in range(16):
+            scatter(p)
 
     mine = core * 8 + z
-    pltpu.make_async_copy(qb.at[mine], qb.at[mine], prec).wait()
-
-
-    @pl.when(y == 0)
-    def _():
-        for d in (4, 3, 5, 2, 6, 1, 7):
-            remote(qb.at[mine], qb.at[mine], p2send.at[d - 1], prec, at(d, z, core), c).start()
-
-    later(y == 0, *[remote(qb.at[0], qb.at[0], p2send.at[d], prec, 0, c) for d in range(7)])
-    for d in (4, 3, 5, 2, 6, 1, 7):
-        remote(qb.at[mine], qb.at[mine], p3send.at[d - 1], p3rec, at(y, (z + d) % NZ, core), c).start()
-    seven = qb.at[pl.ds(0, 7)]
-    pltpu.make_async_copy(seven, seven, p3rec).wait()
-    later(None, *[remote(qb.at[0], qb.at[0], p3send.at[d], p3rec, 0, c) for d in range(7)])
-    half = qb.at[pl.ds(8 * core, 8)]
-    remote(half, half, p4send, p4rec, at(y, z, 1 - core), c).start()
-    other = qb.at[pl.ds(8 * (1 - core), 8)]
-    pltpu.make_async_copy(other, other, p4rec).wait()
-    later(None, remote(half, half, p4send, p4rec, 0, c))
-
-    def quarter(j, t):
-        return con.at[j, pl.ds(256 * t, 256)]
-
-    def send_quarter(t, col, slot):
-        remote(quarter(3, t), quarter(3, t), x3send.at[slot], x3rec.at[t], r, col).start()
-
-    def compute(t):
+    first = c < 2
+
+    def gather(slot, active):
+        @pl.when(active)
+        def _():
+            piece = qb.at[slot, mine]
+            pltpu.make_async_copy(piece, piece, prec.at[slot]).wait()
+
+            @pl.when(y == 0)
+            def _():
+                for d in (4, 3, 5, 2, 6, 1, 7):
+                    remote(piece, piece, p2send.at[slot, d - 1], prec.at[slot], at(d, z, core), c).start()
+
+            for d in (4, 3, 5, 2, 6, 1, 7):
+                remote(piece, piece, p3send.at[slot, d - 1], p3rec.at[slot], at(y, (z + d) % NZ, core), c).start()
+            seven = qb.at[slot, pl.ds(0, 7)]
+            pltpu.make_async_copy(seven, seven, p3rec.at[slot]).wait()
+            half = qb.at[slot, pl.ds(8 * core, 8)]
+            remote(half, half, p4send.at[slot], p4rec.at[slot], at(y, z, 1 - core), c).start()
+            other = qb.at[slot, pl.ds(8 * (1 - core), 8)]
+            pltpu.make_async_copy(other, other, p4rec.at[slot]).wait()
+
+        piece0 = qb.at[0, 0]
+        half0 = qb.at[0, pl.ds(0, 8)]
+        later(active & (y == 0), *[remote(piece0, piece0, p2send.at[slot, d], prec.at[slot], 0, c) for d in range(7)])
+        later(active, *[remote(piece0, piece0, p3send.at[slot, d], p3rec.at[slot], 0, c) for d in range(7)])
+        later(active, remote(half0, half0, p4send.at[slot], p4rec.at[slot], 0, c))
+
+    def compute(k, a_ref, slot, t):
         at_rows = pl.ds(256 * t, 256)
-        b = qb[...].reshape(BS, RHS)
-        con[c, at_rows, :] = jnp.dot(blk[at_rows, :], b, preferred_element_type=F32).astype(BF16)
-
-    @pl.when(c == 3)
-    def _():
-        for t, col in ((0, 0), (2, 2), (1, 0), (3, 2)):
-            compute(t)
-            send_quarter(t, col, t)
-        for t, col in ((2, 0), (0, 2), (3, 0), (1, 2)):
-            send_quarter(t, col, 4 + t)
-
-    @pl.when((c < 3) & jnp.logical_not(early))
+        b = qb[slot].reshape(BS, RHS)
+        con[k, at_rows, :] = jnp.dot(a_ref[at_rows, :], b, preferred_element_type=F32).astype(BF16)
+
+    gather(0, first)
+
+    @pl.when(first & jnp.logical_not(early))
     def _():
         for t in range(4):
-            compute(t)
+            compute(c, blk, 0, t)
 
     for d in (1, 3, 2):
-        @pl.when((c < 3) & jnp.logical_not(support & (c + d == r - 1)))
+        @pl.when(first & jnp.logical_not(support & (c + d == r - 1)))
         def _():
             send_con(d)
 
     later(c < 3, *[remote(con.at[0], con.at[0], xsend.at[d], xrec.at[0], 0, c) for d in range(3)])
-    later(c == 3, *[remote(quarter(3, 0), quarter(3, 0), x3send.at[t], x3rec.at[0], 0, c) for t in range(8)])
-    later((c == 0) | (c == 2), *[remote(quarter(3, 0), quarter(3, 0), x3send.at[t], x3rec.at[0], 0, c) for t in range(2)])
-
-    solved_ref[...] = qb[...].astype(F32).reshape(BS, RHS)
+
+    @pl.when(first)
+    def _():
+        solved_ref[...] = qb[0].astype(F32).reshape(BS, RHS)
+
+    gather(1, c > 0)
+
+    def half_of(h):
+        return con.at[3, pl.ds(512 * h, 512)]
+
+    @pl.when((c == 2) & jnp.logical_not(is_root))
+    def _():
+        for t in range(4):
+            compute(2, blk, 1, t)
+
+    @pl.when(c == 2)
+    def _():
+        for d in (2, 1, 3):
+            send_con(d)
+
+    @pl.when((c == 1) & (r >= 4))
+    def _():
+        pltpu.make_async_copy(blk2, blk2, brec).wait()
+
+    @pl.when((c == 1) & (r < 4))
+    def _():
+        con[3] = jnp.zeros((BS, RHS), BF16)
+
+    for h in range(2):
+        def tiles(which):
+            for t in (2 * which, 2 * which + 1):
+                if h == 0:
+                    @pl.when(r >= 4)
+                    def _():
+                        compute(3, blk2, 1, t)
+                else:
+                    compute(3, blk, 1, t)
+
+        @pl.when(c == 1 + 2 * h)
+        def _():
+            tiles(h)
+            for d in (1, 3):
+                remote(half_of(h), half_of(h), hsend.at[d // 2], hrec.at[h], r, (c + d) % NX).start()
+            tiles(1 - h)
+
+    later(c % 2 == 1, *[remote(half_of(0), half_of(0), hsend.at[d], hrec.at[0], r, 0) for d in range(2)])
+
+    @pl.when(c >= 2)
+    def _():
+        solved_ref[...] = qb[1].astype(F32).reshape(BS, RHS)
 
     for j in range(4):
         @pl.when(c != j)
@@ -347,27 +406,12 @@
 
         update(j, rhs if j == 0 else rem_ref, pl.ds(0, BS))
 
-    for t in (0, 1, 2, 3):
-        @pl.when(c == 0)
-        def _():
-            pltpu.make_async_copy(quarter(3, t), quarter(3, t), x3rec.at[t]).wait()
-            if t < 2:
-                send_quarter(t, 1, t)
-
-        u = (t + 2) % 4
-
-        @pl.when(c == 2)
-        def _():
-            pltpu.make_async_copy(quarter(3, u), quarter(3, u), x3rec.at[u]).wait()
-            if u >= 2:
-                send_quarter(u, 1, u - 2)
-
-        @pl.when(c == 1)
-        def _():
-            v = (0, 2, 1, 3)[t]
-            pltpu.make_async_copy(quarter(3, v), quarter(3, v), x3rec.at[v]).wait()
-
-    update(3, rem_ref, pl.ds(0, BS))
+    for h in range(2):
+        @pl.when(c % 2 == 0)
+        def _():
+            pltpu.make_async_copy(half_of(h), half_of(h), hrec.at[h]).wait()
+
+        update(3, rem_ref, pl.ds(512 * h, 512))
 
     finish()
 
@@ -388,6 +432,7 @@
         scratch_shapes=[
             pltpu.VMEM((2, BS, RHS), F32),
             pltpu.VMEM((BS, BS), BF16),
+            pltpu.VMEM((BS, BS), BF16),
             pltpu.VMEM((32, 8, BS), BF16),
             pltpu.VMEM((128, 8, BS), BF16),
             pltpu.VMEM((BS, BS), BF16),
@@ -396,12 +441,12 @@
             pltpu.VMEM((BS, RHS), BF16),
             pltpu.VMEM((16, PIECE, RHS), BF16),
             pltpu.VMEM((16, PIECE, RHS), BF16),
-            pltpu.VMEM((16, PIECE, RHS), BF16),
+            pltpu.VMEM((2, 16, PIECE, RHS), BF16),
             pltpu.VMEM((4, BS, RHS), BF16),
             pltpu.VMEM((4, 2, 8, RHS), F32),
             dma((2,)), dma((2,)), dma((2,)), dma((8,)), dma((4,)), dma((4,)), dma((4,)),
-            dma((32,)), dma, dma((7,)), dma((7,)), dma, dma, dma,
-            dma((3,)), dma((3,)), dma((8,)), dma((4,)), dma((3,)), dma((4,)),
+            dma((2, 16)), dma((2,)), dma((2, 7)), dma((2, 7)), dma((2,)), dma((2,)), dma((2,)),
+            dma((3,)), dma((4,)), dma((2,)), dma((2,)), dma((3,)), dma((4,)), dma, dma,
         ],
         compiler_params=pltpu.CompilerParams(
             collective_id=0, has_side_effects=True, vmem_limit_bytes=40 << 20

time: 91 us -> 80.1 us (0.88)
  the two profiles are of different devices: /device:TPU:11 before, /device:TPU:9 now
where the time goes in v3:
time: 80.1 us; the launch traced here: 79.8 us
  Pallas kernels  72.5 us (91%)
  local copies, waits for them, and re-layouts  5.41 us (7%)
  between operations  1.94 us (2%)
    pallas_call x1, Pallas kernels, on_device(): pl.pallas_call(kernel, out_shape=(jax.ShapeDtypeStruct((BS, RHS), F32), j...  72.5 us
    unnamed x8, local copies, waits for them, and re-layouts  5.41 us

profile of v3, /device:TPU:9, one launch (start us, length us, event | category | flops | bytes accessed | tf_op | source)
XLA Modules:
  0.0 79.8 jit_solution(581618239517939282)
XLA Ops:
  1.9 0.0 copy-start
  1.9 1.6 %copy-done = bf16[1,1,1,1,1024,1024]{5,4,3,2,1,0:T(8,128)(2,1)S(1)} copy-done((bf16[1,1,1,1,1024,1024]{5,4,3,2,1,0:T(8,128)(2,1)S(1)}, bf16[1,1,1,1,1024,1024]{5,4,3,2,1,0:T(8,128)(2,1)}, u32[]{:S(2)}) %copy-start) | copy-done | bytes 2097176
  3.5 0.0 copy-start.1
  3.5 1.2 %copy-done.1 = f32[2,1,1024,128]{3,2,1,0:T(8,128)S(1)} copy-done((f32[2,1,1024,128]{3,2,1,0:T(8,128)S(1)}, f32[2,1,1024,128]{3,2,1,0:T(8,128)}, u32[]{:S(2)}) %copy-start.1) | copy-done | bytes 1048600
  4.7 0.0 copy-start.2
  4.7 0.8 %copy-done.2 = bf16[4,8,1024]{2,1,0:T(8,128)(2,1)S(1)} copy-done((bf16[4,8,1024]{2,1,0:T(8,128)(2,1)S(1)}, bf16[4,8,1024]{2,1,0:T(8,128)(2,1)}, u32[]{:S(2)}) %copy-start.2) | copy-done | bytes 65560
  5.6 72.5 %shard_map.68 = (f32[1024,128]{1,0:T(8,128)S(1)}, f32[2,1024,128]{2,1,0:T(8,128)S(1)}) custom-call(s32[1]{0:T(128)} %bitcast.8.brow_ref, s32[1]{0:T(128)} %bitcast.9.count_ref, f32[2,1024,128]{2,1,0:T(8,128)S(1)} %bitcast.11, bf16[4,8,1024]{2,1,0:T(8,128)(2,1)S(1)} %copy-done.2, bf16[1024,1024]{1,0:T(8,128)(2,1)S(1)} %bitcast.10), custom_call_target="tpu_custom_call" | custom-call | tf_op jit(solution)/shard_map/pallas_call | solution.py:424
  78.1 0.8 copy.12
  78.9 1.0 %copy.13 = f32[2,1,1024,128]{3,2,1,0:T(8,128)} copy(f32[2,1,1024,128]{3,2,1,0:T(8,128)S(1)} %bitcast.12) | data formatting | bytes 2097152
Async XLA Ops:
  1.9 1.6 %copy-start = (bf16[1,1,1,1,1024,1024]{5,4,3,2,1,0:T(8,128)(2,1)S(1)}, bf16[1,1,1,1,1024,1024]{5,4,3,2,1,0:T(8,128)(2,1)}, u32[]{:S(2)}) copy-start(bf16[1,1,1,1,1024,1024]{5,4,3,2,1,0:T(8,128)(2,1)} %param.7) | copy-start | bytes 6291460
  3.5 1.2 %copy-start.1 = (f32[2,1,1024,128]{3,2,1,0:T(8,128)S(1)}, f32[2,1,1024,128]{3,2,1,0:T(8,128)}, u32[]{:S(2)}) copy-start(f32[2,1,1024,128]{3,2,1,0:T(8,128)} %param.5) | copy-start | bytes 3145732
  4.7 0.8 %copy-start.2 = (bf16[4,8,1024]{2,1,0:T(8,128)(2,1)S(1)}, bf16[4,8,1024]{2,1,0:T(8,128)(2,1)}, u32[]{:S(2)}) copy-start(bf16[4,8,1024]{2,1,0:T(8,128)(2,1)} %diag_hbm.1) | copy-start | bytes 196612

commit v4 on v3

--- a/solution.py
+++ b/solution.py
@@ -12,6 +12,7 @@
 BF16 = jnp.bfloat16
 NY, NZ, NX = 8, 8, 4
 BS, RHS = 1024, 128
+ORDER = (1, 3, 0, 2)
 PIECE = BS // 16
 
 
@@ -22,17 +23,20 @@
     )
 
 
-def kernel(brow_ref, count_ref, rhs_hbm, diag_hbm, blk_hbm, solved_ref, rem_ref,
-           rhs, blk, blk2, dq, dk, dm, own, rhs_left, piv, qc, qn, qb, con, wts,
-           loc, dsend, d0rec, drec, qsend, qrec, fsend, p1send, prec, p2send, p3send, p3rec, p4send, p4rec,
-           xsend, xrec, hsend, hrec, wsend, wrec, bsend, brec):
+def kernel(brow_ref, count_ref, rhs_hbm, diag_hbm, blk_hbm, solved_hbm, rem_hbm,
+           solved_ref, rem_ref, rhs, blk, blk2, dq, dk, dm, own, left, piv, qc, qc2, qn, qb, con, wts,
+           loc, dsend, d0rec, drec, qsend, qrec, q2rec, fsend, p1send, prec, p2send, p3send, p3rec, p4send, p4rec,
+           xsend, xrec, hsend, hrec, wsend, wrec, bsend, brec, turn):
     r = lax.axis_index("row")
     c = lax.axis_index("col")
     core = r % 2
     z = (r // 2) % NZ
     y = r // (2 * NZ)
-    is_root = (c < 3) & (r == c + 1)
-    support = ((c == 0) & ((r == 2) | (r == 3))) | ((c == 1) & (r == 3))
+    is_a = (c == 0) & (r == 1)
+    is_b = (c == 1) & (r == 2)
+    is_c = (c == 1) & (r == 3)
+    is_root = is_a | is_b | is_c
+    support = (c == 0) & ((r == 2) | (r == 3))
     early = is_root | support
     in_quarter = (r // 32) == c
 
@@ -92,9 +96,9 @@
         def _():
             signal(2, 1)
 
-        @pl.when(c % 2 == 1)
-        def _():
-            signal(3, 2)
+        @pl.when((c % 2 == 1) & jnp.logical_not(is_c))
+        def _():
+            signal(3, 1)
 
     for d in range(1, 8):
         signal(at((y + d) % NY, z, core), c)
@@ -104,22 +108,22 @@
     for d in range(1, 4):
         signal(r, (c + d) % NX)
 
+    save_solved = pltpu.make_async_copy(solved_ref, solved_hbm, loc.at[2])
     load_rhs = pltpu.make_async_copy(rhs_hbm, rhs, loc.at[0])
     load_blk = pltpu.make_async_copy(blk_hbm, blk, loc.at[1])
     load_rhs.start()
     load_blk.start()
 
-    k_row = brow_ref[0]
-    glob = k_row * 128 + r
-    valid = (count_ref[0] > 0) & (glob > c)
+    k_row = jnp.broadcast_to(brow_ref[0, 0], (8, RHS))
+    count = jnp.broadcast_to(count_ref[0], (8, RHS))
+    valid = (count > 0) & (k_row * 128 + r > c)
     for i in range(2):
-        w = jnp.where(valid & (k_row == i), F32(1.0), F32(0.0))
-        wts[c, i] = jnp.full((8, RHS), w, F32)
-
-    need = 25 + jnp.where((c < 3) & jnp.logical_not(is_root), 1, 0)
+        wts[c, i] = jnp.where(valid & (k_row == i), F32(1.0), F32(0.0))
+
+    need = 25 + jnp.where(c == 1, 2, jnp.where(c == 0, 1, 0)) - jnp.where(is_root, 1, 0)
     need = need + jnp.where(in_quarter & (r > 0), 1, 0)
     need = need + jnp.where(r == 0, jnp.where(c == 0, 15, 16), 0)
-    need = need + jnp.where(is_root, jnp.where(c == 2, 32, 16), 0)
+    need = need + jnp.where(is_c, 31, jnp.where(is_root, 16, 0))
     pl.semaphore_wait(barrier, need)
 
     for yy in range(NY):
@@ -135,32 +139,47 @@
             def _():
                 pltpu.make_async_copy(diag_hbm.at[0, :, width], dq.at[r % 32, :, width], d0rec.at[yy % 2]).start()
 
-        @pl.when((y == yy) & (c < 3))
-        def _():
-            @pl.when(jnp.logical_not(is_root))
-            def _():
-                remote(diag_hbm.at[c + 1, :, width], dk.at[r, :, width], dsend.at[1], drec.at[yy], c + 1, c).start()
-
-            @pl.when(is_root)
-            def _():
-                pltpu.make_async_copy(diag_hbm.at[c + 1, :, width], dk.at[r, :, width], drec.at[yy]).start()
-
         later((y == yy) & in_quarter & (r > 0),
               remote(diag_hbm.at[0, :, width], dq.at[0, :, width], dsend.at[0], d0rec.at[0], 0, c))
-        later((y == yy) & (c < 3) & jnp.logical_not(is_root),
-              remote(diag_hbm.at[0, :, width], dk.at[0, :, width], dsend.at[1], drec.at[0], 0, c))
-
-    pair = (c == 3) & (r >= 4)
-
-    @pl.when(pair)
-    def _():
-        remote(blk_hbm, blk2, bsend, brec, r, 1).start()
-
-    later(pair, remote(blk_hbm, blk2, bsend, brec, r, 0))
+
+    def send_diag(plane, k, slot):
+        for yy in range(NY):
+            width = pl.ds(0, 128 * (yy + 1))
+            src = diag_hbm.at[k, :, width]
+
+            @pl.when((y == yy) & (c == plane) & (r != k))
+            def _():
+                remote(src, dk.at[r, :, width], dsend.at[slot], drec.at[yy], k, plane).start()
+
+            if yy == 0:
+                @pl.when((c == plane) & (r == k))
+                def _():
+                    pltpu.make_async_copy(src, dk.at[r, :, width], drec.at[yy]).start()
+
+            later((y == yy) & (c == plane) & (r != k),
+                  remote(src, dk.at[0, :, width], dsend.at[slot], drec.at[0], 0, c))
+
+    send_diag(0, 1, 1)
 
     for d in range(1, 4):
         remote(wts.at[c], wts.at[c], wsend.at[d - 1], wrec.at[c], r, (c + d) % NX).start()
 
+    pair = (c == 3) & (r >= 4)
+    lend = (c == 2) & (r == 3)
+
+    @pl.when(pair | lend)
+    def _():
+        remote(blk_hbm, blk2, bsend, brec, r, 1).start()
+
+    later(pair | lend, remote(blk_hbm, blk2, bsend, brec, r, 0))
+
+    for j in range(4):
+        @pl.when(c != j)
+        def _():
+            pltpu.make_async_copy(wts.at[j], wts.at[j], wrec.at[j]).wait()
+
+    send_diag(1, 2, 1)
+    send_diag(1, 3, 2)
     load_rhs.wait()
     load_blk.wait()
 
@@ -215,77 +234,114 @@
             pltpu.make_async_copy(sixteen, sixteen, drec.at[block]).wait()
             dm[pl.ds(128 * block, 128), pl.ds(0, width)] = squeeze(dk, block, width)
 
+    def times(a_ref, q_ref, g, put):
+        b = q_ref[pl.ds(4 * g, 4)].reshape(256, RHS)
+
+        def body(i, carry):
+            at_rows = pl.ds(pl.multiple_of(i * 256, 256), 256)
+            put(at_rows, jnp.dot(a_ref[at_rows, pl.ds(256 * g, 256)], b, preferred_element_type=F32))
+            return carry
+
+        lax.fori_loop(0, 4, body, 0)
+
     @pl.when(early)
     def _():
-        for g in range(4):
+        for n, g in enumerate(ORDER):
             part = pl.ds(4 * g, 4)
             pltpu.make_async_copy(qc.at[part], qc.at[part], qrec.at[g]).wait()
 
-            @pl.when((c == 1) & (r == 2))
+            @pl.when(is_b)
             def _():
                 remote(qc.at[part], qc.at[part], fsend.at[g], qrec.at[g], 3, 1).start()
 
-            b = qc[part].reshape(256, RHS)
-
-            def body(i, carry):
-                at_rows = pl.ds(pl.multiple_of(i * 256, 256), 256)
-                step = jnp.dot(blk[at_rows, pl.ds(256 * g, 256)], b, preferred_element_type=F32)
-                own[at_rows, :] = step if g == 0 else own[at_rows, :] + step
-                return carry
-
-            lax.fori_loop(0, 4, body, 0)
+            def put(at_rows, step):
+                own[at_rows, :] = step if n == 0 else own[at_rows, :] + step
+
+            times(blk, qc, g, put)
+
+    @pl.when(is_a)
+    def _():
+        left[...] = rhs[0] - own[...]
+
+    @pl.when(is_b | is_c)
+    def _():
+        wait_con(0)
+        left[...] = rhs[0] - own[...] - con[0].astype(F32)
+
+    @pl.when(is_c)
+    def _():
+        pltpu.make_async_copy(blk2, blk2, brec).wait()
+        for g in ORDER:
+            part = pl.ds(4 * g, 4)
+            pltpu.make_async_copy(qc2.at[part], qc2.at[part], q2rec.at[g]).wait()
+
+            def put(at_rows, step):
+                left[at_rows, :] = left[at_rows, :] - step
+
+            times(blk2, qc2, g, put)
 
     def scatter(p):
-        k = c + 1
-        slot = k // 2
-        remote(qn.at[p], qb.at[slot, p], p1send.at[0, p], prec.at[slot], line(p), k).start()
-
-        @pl.when(c == 2)
-        def _():
-            remote(qn.at[p], qb.at[slot, p], p1send.at[1, p], prec.at[slot], line(p), 1).start()
+        slot = r // 2
+        remote(qn.at[p], qb.at[slot, p], p1send.at[0, p], prec.at[slot], line(p), r).start()
+
+        @pl.when(is_c)
+        def _():
+            if line(p) == 3:
+                pltpu.make_async_copy(qn.at[p], qb.at[1, p], prec.at[1]).start()
+            else:
+                remote(qn.at[p], qb.at[1, p], p1send.at[1, p], prec.at[1], line(p), 1).start()
 
     @pl.when(is_root)
     def _():
-        def body(j, carry):
-            wait_con(j)
-            rhs_left[...] = rhs_left[...] - con[j].astype(F32)
-            return carry
-
-        rhs_left[...] = rhs[0]
-        lax.fori_loop(0, c, body, 0)
-        piv[...] = (rhs_left[...] - own[...]).astype(BF16)
-        for block in range(8):
-            width = 128 * (block + 1)
-            put_q(block, jnp.dot(dm[pl.ds(128 * block, 128), pl.ds(0, width)], piv[pl.ds(0, width), :],
-                                 preferred_element_type=F32))
-
-            @pl.when(c == 2)
-            def _():
-                for p in (2 * block, 2 * block + 1):
+        piv[...] = left[...].astype(BF16)
+        for g in ORDER:
+            for block in (2 * g, 2 * g + 1):
+                width = 128 * (block + 1)
+                put_q(block, jnp.dot(dm[pl.ds(128 * block, 128), pl.ds(0, width)], piv[pl.ds(0, width), :],
+                                     preferred_element_type=F32))
+
+                @pl.when(is_c)
+                def _():
+                    scatter(2 * block)
+                    scatter(2 * block + 1)
+
+            part = pl.ds(4 * g, 4)
+
+            @pl.when(is_a)
+            def _():
+                remote(qn.at[part], qc.at[part], qsend.at[g], qrec.at[g], 2, 1).start()
+
+            @pl.when(is_b)
+            def _():
+                remote(qn.at[part], qc2.at[part], qsend.at[g], q2rec.at[g], 3, 1).start()
+                for p in range(4 * g, 4 * g + 4):
                     scatter(p)
 
-            if block % 2 == 1:
-                @pl.when(c < 2)
-                def _():
-                    part = pl.ds(2 * block - 2, 4)
-                    remote(qn.at[part], qc.at[part], qsend.at[block // 2], qrec.at[block // 2], c + 2, c + 1).start()
-
-    later((c == 1) & (r == 2), *[remote(qc.at[part0], qc.at[part0], fsend.at[g], qrec.at[0], 0, 0) for g in range(4)])
-    later(is_root & (c < 2), *[remote(qn.at[part0], qc.at[part0], qsend.at[g], qrec.at[0], 0, 0) for g in range(4)])
+    later(is_b, *[remote(qc.at[part0], qc.at[part0], fsend.at[g], qrec.at[0], 0, 0) for g in range(4)])
+    later(is_a | is_b, *[remote(qn.at[part0], qc.at[part0], qsend.at[g], qrec.at[0], 0, 0) for g in range(4)])
     for p in range(16):
         later(is_root, remote(qn.at[p], qb.at[0, p], p1send.at[0, p], prec.at[0], 0, 3))
-        later(is_root & (c == 2), remote(qn.at[p], qb.at[0, p], p1send.at[1, p], prec.at[0], 0, 3))
+        if line(p) != 3:
+            later(is_c, remote(qn.at[p], qb.at[0, p], p1send.at[1, p], prec.at[0], 0, 3))
 
     @pl.when(early)
     def _():
         con[c] = own[...].astype(BF16)
 
-    for d in (1, 2):
-        @pl.when(support & (c + d == r - 1))
-        def _():
-            send_con(d)
-
-    @pl.when(is_root & (c < 2))
+    @pl.when(support)
+    def _():
+        @pl.when(r == 3)
+        def _():
+            pl.semaphore_wait(turn, 1)
+
+        send_con(1)
+
+        @pl.when(r == 2)
+        def _():
+            remote(con.at[0], con.at[0], xsend.at[0], xrec.at[0], 0, c).wait_send()
+            pl.semaphore_signal(turn, inc=1, device_id={"row": 3, "col": 0}, device_id_type=MESH)
+
+    @pl.when(is_a)
     def _():
         for p in range(16):
             scatter(p)
@@ -332,22 +388,24 @@
             compute(c, blk, 0, t)
 
     for d in (1, 3, 2):
-        @pl.when(first & jnp.logical_not(support & (c + d == r - 1)))
+        @pl.when(first & jnp.logical_not(support & (d == 1)))
         def _():
             send_con(d)
 
-    later(c < 3, *[remote(con.at[0], con.at[0], xsend.at[d], xrec.at[0], 0, c) for d in range(3)])
+    later((c < 3) & ((c > 0) | (r != 2)), remote(con.at[0], con.at[0], xsend.at[0], xrec.at[0], 0, c))
+    later(c < 3, *[remote(con.at[0], con.at[0], xsend.at[d], xrec.at[0], 0, c) for d in (1, 2)])
 
     @pl.when(first)
     def _():
         solved_ref[...] = qb[0].astype(F32).reshape(BS, RHS)
+        save_solved.start()
 
     gather(1, c > 0)
 
-    def half_of(h):
-        return con.at[3, pl.ds(512 * h, 512)]
-
-    @pl.when((c == 2) & jnp.logical_not(is_root))
+    def tile_of(t):
+        return con.at[3, pl.ds(256 * t, 256)]
+
+    @pl.when(c == 2)
     def _():
         for t in range(4):
             compute(2, blk, 1, t)
@@ -366,32 +424,29 @@
         con[3] = jnp.zeros((BS, RHS), BF16)
 
     for h in range(2):
-        def tiles(which):
-            for t in (2 * which, 2 * which + 1):
-                if h == 0:
-                    @pl.when(r >= 4)
-                    def _():
-                        compute(3, blk2, 1, t)
-                else:
-                    compute(3, blk, 1, t)
+        def tile(t):
+            if h == 0:
+                @pl.when(r >= 4)
+                def _():
+                    compute(3, blk2, 1, t)
+            else:
+                compute(3, blk, 1, t)
 
         @pl.when(c == 1 + 2 * h)
         def _():
-            tiles(h)
-            for d in (1, 3):
-                remote(half_of(h), half_of(h), hsend.at[d // 2], hrec.at[h], r, (c + d) % NX).start()
-            tiles(1 - h)
-
-    later(c % 2 == 1, *[remote(half_of(0), half_of(0), hsend.at[d], hrec.at[0], r, 0) for d in range(2)])
+            for t in (2 * h, 2 * h + 1):
+                tile(t)
+                for d in (1, 3):
+                    remote(tile_of(t), tile_of(t), hsend.at[d // 2, t % 2], hrec.at[t], r, (c + d) % NX).start()
+            for t in (2 - 2 * h, 3 - 2 * h):
+                tile(t)
+
+    later(c % 2 == 1, *[remote(tile_of(0), tile_of(0), hsend.at[d, t], hrec.at[0], r, 0) for d in range(2) for t in range(2)])
 
     @pl.when(c >= 2)
     def _():
         solved_ref[...] = qb[1].astype(F32).reshape(BS, RHS)
-
-    for j in range(4):
-        @pl.when(c != j)
-        def _():
-            pltpu.make_async_copy(wts.at[j], wts.at[j], wrec.at[j]).wait()
+        save_solved.start()
 
     def update(j, base, rows):
         got = con[j, rows, :].astype(F32).reshape(rows.size // 8, 8, RHS)
@@ -400,25 +455,46 @@
             rem_ref[i, rows, :] = base[i, rows, :] - step
 
     for j in range(3):
-        @pl.when((c != j) & jnp.logical_not(is_root & (c > j)))
+        @pl.when((c != j) & jnp.logical_not((is_b | is_c) & (j == 0)))
         def _():
             wait_con(j)
 
         update(j, rhs if j == 0 else rem_ref, pl.ds(0, BS))
 
-    for h in range(2):
+    for n, t in enumerate((0, 2, 1, 3)):
         @pl.when(c % 2 == 0)
         def _():
-            pltpu.make_async_copy(half_of(h), half_of(h), hrec.at[h]).wait()
-
-        update(3, rem_ref, pl.ds(512 * h, 512))
-
+            pltpu.make_async_copy(tile_of(t), tile_of(t), hrec.at[t]).wait()
+
+        rows = pl.ds(256 * t, 256)
+        update(3, rem_ref, rows)
+        pltpu.make_async_copy(rem_ref.at[:, rows], rem_hbm.at[:, rows], loc.at[3 + t]).start()
+
+    for t in range(4):
+        rows = pl.ds(256 * t, 256)
+        pltpu.make_async_copy(rem_ref.at[:, rows], rem_hbm.at[:, rows], loc.at[3 + t]).wait()
+    save_solved.wait()
     finish()
+
+
+def hand_over(solved_in, rem_in, solved_out, rem_out, buf, sems):
+    moves = [(solved_in, solved_out)]
+    moves += [(rem_in.at[i], rem_out.at[i, 0]) for i in range(2)]
+    moves = [(a.at[pl.ds(512 * h, 512)], (b.at[0, 0] if n == 0 else b).at[pl.ds(512 * h, 512)])
+             for n, (a, b) in enumerate(moves) for h in range(2)]
+    reads = [pltpu.make_async_copy(a, buf.at[n], sems.at[0, n]) for n, (a, b) in enumerate(moves)]
+    writes = [pltpu.make_async_copy(buf.at[n], b, sems.at[1, n]) for n, (a, b) in enumerate(moves)]
+    for read in reads:
+        read.start()
+    for read, write in zip(reads, writes):
+        read.wait()
+        write.start()
+    for write in writes:
+        write.wait()
 
 
 def on_device(rhs, diag_inv, blocks, block_rows, counts):
     vmem = pl.BlockSpec(memory_space=pltpu.VMEM)
-    smem = pl.BlockSpec(memory_space=pltpu.SMEM)
     hbm = pl.BlockSpec(memory_space=pltpu.HBM)
     dma = pltpu.SemaphoreType.DMA
     solved, rem = pl.pallas_call(
@@ -427,9 +503,11 @@
             jax.ShapeDtypeStruct((BS, RHS), F32),
             jax.ShapeDtypeStruct((2, BS, RHS), F32),
         ),
-        in_specs=[smem, smem, hbm, hbm, hbm],
-        out_specs=(vmem, vmem),
+        in_specs=[vmem, vmem, hbm, hbm, hbm],
+        out_specs=(hbm, hbm),
         scratch_shapes=[
+            pltpu.VMEM((BS, RHS), F32),
+            pltpu.VMEM((2, BS, RHS), F32),
             pltpu.VMEM((2, BS, RHS), F32),
             pltpu.VMEM((BS, BS), BF16),
             pltpu.VMEM((BS, BS), BF16),
@@ -441,21 +519,32 @@
             pltpu.VMEM((BS, RHS), BF16),
             pltpu.VMEM((16, PIECE, RHS), BF16),
             pltpu.VMEM((16, PIECE, RHS), BF16),
+            pltpu.VMEM((16, PIECE, RHS), BF16),
             pltpu.VMEM((2, 16, PIECE, RHS), BF16),
             pltpu.VMEM((4, BS, RHS), BF16),
             pltpu.VMEM((4, 2, 8, RHS), F32),
-            dma((2,)), dma((2,)), dma((2,)), dma((8,)), dma((4,)), dma((4,)), dma((4,)),
+            dma((7,)), dma((3,)), dma((2,)), dma((8,)), dma((4,)), dma((4,)), dma((4,)), dma((4,)),
             dma((2, 16)), dma((2,)), dma((2, 7)), dma((2, 7)), dma((2,)), dma((2,)), dma((2,)),
-            dma((3,)), dma((4,)), dma((2,)), dma((2,)), dma((3,)), dma((4,)), dma, dma,
+            dma((3,)), dma((4,)), dma((2, 2)), dma((4,)), dma((3,)), dma((4,)), dma, dma, pltpu.SemaphoreType.REGULAR,
         ],
         compiler_params=pltpu.CompilerParams(
-            collective_id=0, has_side_effects=True, vmem_limit_bytes=40 << 20
+            collective_id=0, has_side_effects=True, vmem_limit_bytes=63 << 20
         ),
     )(
-        block_rows.reshape(1), counts.reshape(1), rhs.reshape(2, BS, RHS), diag_inv,
+        block_rows, counts, rhs.reshape(2, BS, RHS), diag_inv,
         blocks.reshape(BS, BS),
     )
-    return solved.reshape(1, 1, BS, RHS), rem.reshape(2, 1, BS, RHS)
+    return pl.pallas_call(
+        hand_over,
+        out_shape=(
+            jax.ShapeDtypeStruct((1, 1, BS, RHS), F32),
+            jax.ShapeDtypeStruct((2, 1, BS, RHS), F32),
+        ),
+        in_specs=[hbm, hbm],
+        out_specs=(hbm, hbm),
+        scratch_shapes=[pltpu.VMEM((6, BS // 2, RHS), F32), dma((2, 6))],
+        compiler_params=pltpu.CompilerParams(vmem_limit_bytes=63 << 20),
+    )(solved, rem)
 
 
 def solution(mesh):

time: 80.1 us -> 74.5 us (0.930)
  local copies, waits for them, and re-layouts: 5.41 us -> 0 us
    unnamed x8 -> x0, local copies, waits for them, and re-layouts: 5.41 us -> none
    pallas_call x1, Pallas kernels: 72.5 us -> 69.5 us  [on_device(): pl.pallas_call(kernel, out_shape=(jax.ShapeDtypeStruct((BS, RHS), F32), j...]
    pallas_call x0 -> x1, Pallas kernels: none -> 2.19 us  [on_device(): pl.pallas_call(hand_over, out_shape=(jax.ShapeDtypeStruct((1, 1, BS, RHS)...]
where the time goes in v4:
time: 74.5 us; the launch traced here: 73.6 us
  Pallas kernels  71.7 us (96%)
  between operations  1.93 us (3%)
    pallas_call x1, Pallas kernels, on_device(): pl.pallas_call(kernel, out_shape=(jax.ShapeDtypeStruct((BS, RHS), F32), j...  69.5 us
    pallas_call x1, Pallas kernels, on_device(): pl.pallas_call(hand_over, out_shape=(jax.ShapeDtypeStruct((1, 1, BS, RHS)...  2.19 us

profile of v4, /device:TPU:9, one launch (start us, length us, event | category | flops | bytes accessed | tf_op | source)
XLA Modules:
  0.0 73.6 jit_solution(1723512031276647223)
XLA Ops:
  1.9 69.5 %shard_map.68 = (f32[1024,128]{1,0:T(8,128)}, f32[2,1024,128]{2,1,0:T(8,128)}) custom-call(s32[1,1,1,1]{3,2,1,0:T(1,128)S(6)} %copy.7.brow_ref, s32[1,1,1]{2,1,0:T(1,128)S(6)} %copy.8.count_ref, f32[2,1024,128]{2,1,0:T(8,128)} %bitcast.3, bf16[4,8,1024]{2,1,0:T(8,128)(2,1)} %diag_hbm.1, bf16[1024,1024]{1,0:T(8,128)(2,1)} %bitcast.2), custom_call_target="tpu_custom_call" | custom-call | tf_op jit(solution)/shard_map/pallas_call | solution.py:500
  71.4 2.2 %shard_map.69 = (f32[1,1,1024,128]{3,2,1,0:T(8,128)}, f32[2,1,1024,128]{3,2,1,0:T(8,128)}) custom-call(f32[1024,128]{1,0:T(8,128)} %get-tuple-element.4.solved_in, f32[2,1024,128]{2,1,0:T(8,128)} %get-tuple-element.5.rem_in), custom_call_target="tpu_custom_call" | custom-call | tf_op jit(solution)/shard_map/pallas_call | solution.py:537

commit v5 on v4

--- a/solution.py
+++ b/solution.py
@@ -23,8 +23,8 @@
     )
 
 
-def kernel(brow_ref, count_ref, rhs_hbm, diag_hbm, blk_hbm, solved_hbm, rem_hbm,
-           solved_ref, rem_ref, rhs, blk, blk2, dq, dk, dm, own, left, piv, qc, qc2, qn, qb, con, wts,
+def kernel(brow_ref, count_ref, rhs_hbm, diag_hbm, blk_hbm, solved_ref, rem_ref,
+           rhs, blk, blk2, dq, dk, dm, own, left, piv, qc, qc2, qn, qb, con, wts,
            loc, dsend, d0rec, drec, qsend, qrec, q2rec, fsend, p1send, prec, p2send, p3send, p3rec, p4send, p4rec,
            xsend, xrec, hsend, hrec, wsend, wrec, bsend, brec, turn):
     r = lax.axis_index("row")
@@ -108,7 +108,6 @@
     for d in range(1, 4):
         signal(r, (c + d) % NX)
 
-    save_solved = pltpu.make_async_copy(solved_ref, solved_hbm, loc.at[2])
     load_rhs = pltpu.make_async_copy(rhs_hbm, rhs, loc.at[0])
     load_blk = pltpu.make_async_copy(blk_hbm, blk, loc.at[1])
     load_rhs.start()
@@ -398,7 +397,6 @@
     @pl.when(first)
     def _():
         solved_ref[...] = qb[0].astype(F32).reshape(BS, RHS)
-        save_solved.start()
 
     gather(1, c > 0)
 
@@ -446,7 +444,6 @@
     @pl.when(c >= 2)
     def _():
         solved_ref[...] = qb[1].astype(F32).reshape(BS, RHS)
-        save_solved.start()
 
     def update(j, base, rows):
         got = con[j, rows, :].astype(F32).reshape(rows.size // 8, 8, RHS)
@@ -466,48 +463,35 @@
         def _():
             pltpu.make_async_copy(tile_of(t), tile_of(t), hrec.at[t]).wait()
 
-        rows = pl.ds(256 * t, 256)
-        update(3, rem_ref, rows)
-        pltpu.make_async_copy(rem_ref.at[:, rows], rem_hbm.at[:, rows], loc.at[3 + t]).start()
-
-    for t in range(4):
-        rows = pl.ds(256 * t, 256)
-        pltpu.make_async_copy(rem_ref.at[:, rows], rem_hbm.at[:, rows], loc.at[3 + t]).wait()
-    save_solved.wait()
+        update(3, rem_ref, pl.ds(256 * t, 256))
+
     finish()
 
 
-def hand_over(solved_in, rem_in, solved_out, rem_out, buf, sems):
-    moves = [(solved_in, solved_out)]
-    moves += [(rem_in.at[i], rem_out.at[i, 0]) for i in range(2)]
-    moves = [(a.at[pl.ds(512 * h, 512)], (b.at[0, 0] if n == 0 else b).at[pl.ds(512 * h, 512)])
-             for n, (a, b) in enumerate(moves) for h in range(2)]
-    reads = [pltpu.make_async_copy(a, buf.at[n], sems.at[0, n]) for n, (a, b) in enumerate(moves)]
-    writes = [pltpu.make_async_copy(buf.at[n], b, sems.at[1, n]) for n, (a, b) in enumerate(moves)]
-    for read in reads:
-        read.start()
-    for read, write in zip(reads, writes):
-        read.wait()
-        write.start()
-    for write in writes:
-        write.wait()
+def hand_over(solved_in, rem_in, solved_out, rem_out, sems):
+    pairs = [(rem_in.at[0], rem_out.at[0, 0]), (rem_in.at[1], rem_out.at[1, 0]), (solved_in, solved_out.at[0, 0])]
+    moves = []
+    for n, (src, dst) in enumerate(pairs):
+        for t in range(4):
+            rows = pl.ds(256 * t, 256)
+            moves.append(pltpu.make_async_copy(src.at[rows], dst.at[rows], sems.at[n, t]))
+    for move in moves:
+        move.start()
+    for move in moves:
+        move.wait()
 
 
 def on_device(rhs, diag_inv, blocks, block_rows, counts):
     vmem = pl.BlockSpec(memory_space=pltpu.VMEM)
     hbm = pl.BlockSpec(memory_space=pltpu.HBM)
     dma = pltpu.SemaphoreType.DMA
+    here = pltpu.with_memory_space_constraint
     solved, rem = pl.pallas_call(
         kernel,
-        out_shape=(
-            jax.ShapeDtypeStruct((BS, RHS), F32),
-            jax.ShapeDtypeStruct((2, BS, RHS), F32),
-        ),
+        out_shape=(pltpu.VMEM((BS, RHS), F32), pltpu.VMEM((2, BS, RHS), F32)),
         in_specs=[vmem, vmem, hbm, hbm, hbm],
-        out_specs=(hbm, hbm),
+        out_specs=(vmem, vmem),
         scratch_shapes=[
-            pltpu.VMEM((BS, RHS), F32),
-            pltpu.VMEM((2, BS, RHS), F32),
             pltpu.VMEM((2, BS, RHS), F32),
             pltpu.VMEM((BS, BS), BF16),
             pltpu.VMEM((BS, BS), BF16),
@@ -523,16 +507,16 @@
             pltpu.VMEM((2, 16, PIECE, RHS), BF16),
             pltpu.VMEM((4, BS, RHS), BF16),
             pltpu.VMEM((4, 2, 8, RHS), F32),
-            dma((7,)), dma((3,)), dma((2,)), dma((8,)), dma((4,)), dma((4,)), dma((4,)), dma((4,)),
+            dma((2,)), dma((3,)), dma((2,)), dma((8,)), dma((4,)), dma((4,)), dma((4,)), dma((4,)),
             dma((2, 16)), dma((2,)), dma((2, 7)), dma((2, 7)), dma((2,)), dma((2,)), dma((2,)),
             dma((3,)), dma((4,)), dma((2, 2)), dma((4,)), dma((3,)), dma((4,)), dma, dma, pltpu.SemaphoreType.REGULAR,
         ],
         compiler_params=pltpu.CompilerParams(
-            collective_id=0, has_side_effects=True, vmem_limit_bytes=63 << 20
+            collective_id=0, has_side_effects=True, vmem_limit_bytes=40 << 20
         ),
     )(
-        block_rows, counts, rhs.reshape(2, BS, RHS), diag_inv,
-        blocks.reshape(BS, BS),
+        block_rows, counts, here(rhs.reshape(2, BS, RHS), pltpu.HBM), here(diag_inv, pltpu.HBM),
+        here(blocks.reshape(BS, BS), pltpu.HBM),
     )
     return pl.pallas_call(
         hand_over,
@@ -540,11 +524,11 @@
             jax.ShapeDtypeStruct((1, 1, BS, RHS), F32),
             jax.ShapeDtypeStruct((2, 1, BS, RHS), F32),
         ),
-        in_specs=[hbm, hbm],
+        in_specs=[vmem, vmem],
         out_specs=(hbm, hbm),
-        scratch_shapes=[pltpu.VMEM((6, BS // 2, RHS), F32), dma((2, 6))],
-        compiler_params=pltpu.CompilerParams(vmem_limit_bytes=63 << 20),
-    )(solved, rem)
+        scratch_shapes=[dma((3, 4))],
+        compiler_params=pltpu.CompilerParams(vmem_limit_bytes=4 << 20),
+    )(here(solved, pltpu.VMEM), here(rem, pltpu.VMEM))
 
 
 def solution(mesh):

time: 74.5 us -> 72.9 us (0.979)
  Pallas kernels: 71.7 us -> 70.1 us
    pallas_call x1, Pallas kernels: 2.19 us -> 1.23 us  [on_device(): pl.pallas_call(hand_over, out_shape=(jax.ShapeDtypeStruct((1, 1, BS, RHS)...]
where the time goes in v5:
time: 72.9 us; the launch traced here: 72 us
  Pallas kernels  70.1 us (96%)
  between operations  1.93 us (3%)
    pallas_call x1, Pallas kernels, on_device(): pl.pallas_call(kernel, out_shape=(pltpu.VMEM((BS, RHS), F32), pltpu.VMEM(...  68.9 us

profile of v5, /device:TPU:9, one launch (start us, length us, event | category | flops | bytes accessed | tf_op | source)
XLA Modules:
  0.0 72.0 jit_solution(15981807252358127331)
XLA Ops:
  1.9 68.9 %shard_map.68 = (f32[1024,128]{1,0:T(8,128)S(1)}, f32[2,1024,128]{2,1,0:T(8,128)S(1)}) custom-call(s32[1,1,1,1]{3,2,1,0:T(1,128)S(6)} %copy.7.brow_ref, s32[1,1,1]{2,1,0:T(1,128)S(6)} %copy.8.count_ref, f32[2,1024,128]{2,1,0:T(8,128)} %bitcast.3, bf16[4,8,1024]{2,1,0:T(8,128)(2,1)} %diag_hbm.1, bf16[1024,1024]{1,0:T(8,128)(2,1)} %bitcast.2), custom_call_target="tpu_custom_call" | custom-call | tf_op jit(solution)/shard_map/pallas_call | solution.py:489
  70.8 1.2 %shard_map.69 = (f32[1,1,1024,128]{3,2,1,0:T(8,128)}, f32[2,1,1024,128]{3,2,1,0:T(8,128)}) custom-call(f32[1024,128]{1,0:T(8,128)S(1)} %get-tuple-element.4.solved_in, f32[2,1024,128]{2,1,0:T(8,128)S(1)} %get-tuple-element.5.rem_in), custom_call_target="tpu_custom_call" | custom-call | tf_op jit(solution)/shard_map/pallas_call | solution.py:521

commit v6 on v5

--- a/solution.py
+++ b/solution.py
@@ -26,7 +26,7 @@
 def kernel(brow_ref, count_ref, rhs_hbm, diag_hbm, blk_hbm, solved_ref, rem_ref,
            rhs, blk, blk2, dq, dk, dm, own, left, piv, qc, qc2, qn, qb, con, wts,
            loc, dsend, d0rec, drec, qsend, qrec, q2rec, fsend, p1send, prec, p2send, p3send, p3rec, p4send, p4rec,
-           xsend, xrec, hsend, hrec, wsend, wrec, bsend, brec, turn):
+           xsend, xrec, h1send, h1rec, hsend, hrec, wsend, wrec, bsend, brec, turn):
     r = lax.axis_index("row")
     c = lax.axis_index("col")
     core = r % 2
@@ -88,7 +88,7 @@
                 def _():
                     signal(0, cc)
 
-        @pl.when(c == 1)
+        @pl.when(c % 2 == 1)
         def _():
             signal(1, 0)
 
@@ -122,7 +122,7 @@
     need = 25 + jnp.where(c == 1, 2, jnp.where(c == 0, 1, 0)) - jnp.where(is_root, 1, 0)
     need = need + jnp.where(in_quarter & (r > 0), 1, 0)
     need = need + jnp.where(r == 0, jnp.where(c == 0, 15, 16), 0)
-    need = need + jnp.where(is_c, 31, jnp.where(is_root, 16, 0))
+    need = need + jnp.where(is_c, 31, jnp.where(is_a, 32, jnp.where(is_root, 16, 0)))
     pl.semaphore_wait(barrier, need)
 
     for yy in range(NY):
@@ -165,12 +165,18 @@
 
     pair = (c == 3) & (r >= 4)
     lend = (c == 2) & (r == 3)
+    lower = pl.ds(512, 512)
 
     @pl.when(pair | lend)
     def _():
         remote(blk_hbm, blk2, bsend, brec, r, 1).start()
 
+    @pl.when((c == 1) & (r >= 4))
+    def _():
+        remote(blk_hbm.at[lower], blk2.at[lower], bsend, brec, r, 3).start()
+
     later(pair | lend, remote(blk_hbm, blk2, bsend, brec, r, 0))
+    later((c == 1) & (r >= 4), remote(blk_hbm.at[lower], blk2.at[lower], bsend, brec, r, 0))
 
     for j in range(4):
         @pl.when(c != j)
@@ -283,6 +289,10 @@
         slot = r // 2
         remote(qn.at[p], qb.at[slot, p], p1send.at[0, p], prec.at[slot], line(p), r).start()
 
+        @pl.when(is_a)
+        def _():
+            remote(qn.at[p], qb.at[0, p], p1send.at[1, p], prec.at[0], line(p), 3).start()
+
         @pl.when(is_c)
         def _():
             if line(p) == 3:
@@ -320,6 +330,7 @@
     later(is_a | is_b, *[remote(qn.at[part0], qc.at[part0], qsend.at[g], qrec.at[0], 0, 0) for g in range(4)])
     for p in range(16):
         later(is_root, remote(qn.at[p], qb.at[0, p], p1send.at[0, p], prec.at[0], 0, 3))
+        later(is_a, remote(qn.at[p], qb.at[0, p], p1send.at[1, p], prec.at[0], 0, 3))
         if line(p) != 3:
             later(is_c, remote(qn.at[p], qb.at[0, p], p1send.at[1, p], prec.at[0], 0, 3))
 
@@ -379,29 +390,66 @@
         b = qb[slot].reshape(BS, RHS)
         con[k, at_rows, :] = jnp.dot(a_ref[at_rows, :], b, preferred_element_type=F32).astype(BF16)
 
-    gather(0, first)
-
-    @pl.when(first & jnp.logical_not(early))
+    def tile_of(k, t):
+        return con.at[k, pl.ds(256 * t, 256)]
+
+    def share(k, plane, a_ref, slot, which, sends, recs):
+        @pl.when((c == plane) & which)
+        def _():
+            h = plane // 2
+            for t in (2 * h, 2 * h + 1):
+                compute(k, a_ref, slot, t)
+                for d in (1, 3):
+                    remote(tile_of(k, t), tile_of(k, t), sends.at[d // 2, t % 2], recs.at[t], r, (c + d) % NX).start()
+            for t in (2 - 2 * h, 3 - 2 * h):
+                compute(k, a_ref, slot, t)
+
+    gather(0, c != 2)
+    low = r < 4
+    high = r >= 4
+
+    @pl.when(first & jnp.logical_not(early) & ((c == 0) | low))
     def _():
         for t in range(4):
             compute(c, blk, 0, t)
 
     for d in (1, 3, 2):
-        @pl.when(first & jnp.logical_not(support & (d == 1)))
+        @pl.when(first & ((c == 0) | low) & jnp.logical_not(support & (d == 1)))
         def _():
             send_con(d)
 
-    later((c < 3) & ((c > 0) | (r != 2)), remote(con.at[0], con.at[0], xsend.at[0], xrec.at[0], 0, c))
-    later(c < 3, *[remote(con.at[0], con.at[0], xsend.at[d], xrec.at[0], 0, c) for d in (1, 2)])
+    whole = (c == 0) | (c == 2) | ((c == 1) & low)
+    later(whole & ((c > 0) | (r != 2)), remote(con.at[0], con.at[0], xsend.at[0], xrec.at[0], 0, c))
+    later(whole, *[remote(con.at[0], con.at[0], xsend.at[d], xrec.at[0], 0, c) for d in (1, 2)])
+    def give(t, d):
+        remote(tile_of(1, t), tile_of(1, t), h1send.at[d - 1, t % 2], h1rec.at[t], r, (c + d) % NX).start()
+
+    @pl.when((c == 1) & high)
+    def _():
+        for t in (0, 1):
+            compute(1, blk, 0, t)
+            for d in (2, 1, 3):
+                give(t, d)
+        for t in (2, 3):
+            compute(1, blk, 0, t)
+
+    @pl.when((c == 3) & high)
+    def _():
+        pltpu.make_async_copy(blk2.at[lower], blk2.at[lower], brec).wait()
+        for t in (2, 3):
+            compute(1, blk2, 0, t)
+            for d in (1, 3):
+                give(t, d)
+
+    tile0 = tile_of(1, 0)
+    later((c % 2 == 1) & high, *[remote(tile0, tile0, h1send.at[d, t], h1rec.at[0], r, 0) for d in (0, 2) for t in range(2)])
+    later((c == 1) & high, *[remote(tile0, tile0, h1send.at[1, t], h1rec.at[0], r, 0) for t in range(2)])
 
     @pl.when(first)
     def _():
         solved_ref[...] = qb[0].astype(F32).reshape(BS, RHS)
 
     gather(1, c > 0)
-
-    def tile_of(t):
-        return con.at[3, pl.ds(256 * t, 256)]
 
     @pl.when(c == 2)
     def _():
@@ -421,25 +469,16 @@
     def _():
         con[3] = jnp.zeros((BS, RHS), BF16)
 
-    for h in range(2):
-        def tile(t):
-            if h == 0:
-                @pl.when(r >= 4)
-                def _():
-                    compute(3, blk2, 1, t)
-            else:
-                compute(3, blk, 1, t)
-
-        @pl.when(c == 1 + 2 * h)
-        def _():
-            for t in (2 * h, 2 * h + 1):
-                tile(t)
-                for d in (1, 3):
-                    remote(tile_of(t), tile_of(t), hsend.at[d // 2, t % 2], hrec.at[t], r, (c + d) % NX).start()
-            for t in (2 - 2 * h, 3 - 2 * h):
-                tile(t)
-
-    later(c % 2 == 1, *[remote(tile_of(0), tile_of(0), hsend.at[d, t], hrec.at[0], r, 0) for d in range(2) for t in range(2)])
+    share(3, 1, blk2, 1, high, hsend, hrec)
+
+    @pl.when((c == 1) & low)
+    def _():
+        for t in (0, 1):
+            for d in (1, 3):
+                remote(tile_of(3, t), tile_of(3, t), hsend.at[d // 2, t], hrec.at[t], r, (c + d) % NX).start()
+
+    share(3, 3, blk, 1, c == 3, hsend, hrec)
+    later(c % 2 == 1, *[remote(tile_of(3, 0), tile_of(3, 0), hsend.at[d, t], hrec.at[0], r, 0) for d in range(2) for t in range(2)])
 
     @pl.when(c >= 2)
     def _():
@@ -452,16 +491,24 @@
             rem_ref[i, rows, :] = base[i, rows, :] - step
 
     for j in range(3):
-        @pl.when((c != j) & jnp.logical_not((is_b | is_c) & (j == 0)))
+        waits = (c != j) & jnp.logical_not((is_b | is_c) & (j == 0))
+
+        @pl.when(waits & (low if j == 1 else c >= 0))
         def _():
             wait_con(j)
+
+        if j == 1:
+            for t in range(4):
+                @pl.when((c != 1 if t < 2 else c % 2 == 0) & high)
+                def _():
+                    pltpu.make_async_copy(tile_of(1, t), tile_of(1, t), h1rec.at[t]).wait()
 
         update(j, rhs if j == 0 else rem_ref, pl.ds(0, BS))
 
     for n, t in enumerate((0, 2, 1, 3)):
         @pl.when(c % 2 == 0)
         def _():
-            pltpu.make_async_copy(tile_of(t), tile_of(t), hrec.at[t]).wait()
+            pltpu.make_async_copy(tile_of(3, t), tile_of(3, t), hrec.at[t]).wait()
 
         update(3, rem_ref, pl.ds(256 * t, 256))
 
@@ -509,7 +556,7 @@
             pltpu.VMEM((4, 2, 8, RHS), F32),
             dma((2,)), dma((3,)), dma((2,)), dma((8,)), dma((4,)), dma((4,)), dma((4,)), dma((4,)),
             dma((2, 16)), dma((2,)), dma((2, 7)), dma((2, 7)), dma((2,)), dma((2,)), dma((2,)),
-            dma((3,)), dma((4,)), dma((2, 2)), dma((4,)), dma((3,)), dma((4,)), dma, dma, pltpu.SemaphoreType.REGULAR,
+            dma((3,)), dma((4,)), dma((3, 2)), dma((4,)), dma((2, 2)), dma((4,)), dma((3,)), dma((4,)), dma, dma, pltpu.SemaphoreType.REGULAR,
         ],
         compiler_params=pltpu.CompilerParams(
             collective_id=0, has_side_effects=True, vmem_limit_bytes=40 << 20

time: 72.9 us -> 71.6 us (0.982); the launches traced: 72 us -> 71.5 us
  no operation moved by 1% of the time
where the time goes in v6:
time: 71.6 us; the launch traced here: 71.5 us
  Pallas kernels  69.5 us (97%)
  between operations  1.93 us (3%)
    pallas_call x1, Pallas kernels, on_device(): pl.pallas_call(kernel, out_shape=(pltpu.VMEM((BS, RHS), F32), pltpu.VMEM(...  68.3 us

profile of v6, /device:TPU:9, one launch (start us, length us, event | category | flops | bytes accessed | tf_op | source)
XLA Modules:
  0.0 71.5 jit_solution(14414136104549678472)
XLA Ops:
  1.9 68.3 %shard_map.68 = (f32[1024,128]{1,0:T(8,128)S(1)}, f32[2,1024,128]{2,1,0:T(8,128)S(1)}) custom-call(s32[1,1,1,1]{3,2,1,0:T(1,128)S(6)} %copy.7.brow_ref, s32[1,1,1]{2,1,0:T(1,128)S(6)} %copy.8.count_ref, f32[2,1024,128]{2,1,0:T(8,128)} %bitcast.3, bf16[4,8,1024]{2,1,0:T(8,128)(2,1)} %diag_hbm.1, bf16[1024,1024]{1,0:T(8,128)(2,1)} %bitcast.2), custom_call_target="tpu_custom_call" | custom-call | tf_op jit(solution)/shard_map/pallas_call | solution.py:536
  70.2 1.2 %shard_map.69 = (f32[1,1,1024,128]{3,2,1,0:T(8,128)}, f32[2,1,1024,128]{3,2,1,0:T(8,128)}) custom-call(f32[1024,128]{1,0:T(8,128)S(1)} %get-tuple-element.4.solved_in, f32[2,1024,128]{2,1,0:T(8,128)S(1)} %get-tuple-element.5.rem_in), custom_call_target="tpu_custom_call" | custom-call | tf_op jit(solution)/shard_map/pallas_call | solution.py:568

commit v7 on v6

--- a/solution.py
+++ b/solution.py
@@ -12,7 +12,7 @@
 BF16 = jnp.bfloat16
 NY, NZ, NX = 8, 8, 4
 BS, RHS = 1024, 128
-ORDER = (1, 3, 0, 2)
+ORDER = (0, 2, 1, 3)
 PIECE = BS // 16
 
 

time: 71.6 us -> 70.4 us (0.983)
  Pallas kernels: 69.5 us -> 68.4 us
    pallas_call x1, Pallas kernels: 68.3 us -> 67.1 us  [on_device(): pl.pallas_call(kernel, out_shape=(pltpu.VMEM((BS, RHS), F32), pltpu.VMEM(...]
where the time goes in v7:
time: 70.4 us; the launch traced here: 70.3 us
  Pallas kernels  68.4 us (97%)
  between operations  1.93 us (3%)
    pallas_call x1, Pallas kernels, on_device(): pl.pallas_call(kernel, out_shape=(pltpu.VMEM((BS, RHS), F32), pltpu.VMEM(...  67.1 us

profile of v7, /device:TPU:9, one launch (start us, length us, event | category | flops | bytes accessed | tf_op | source)
XLA Modules:
  0.0 70.3 jit_solution(1099425769747686421)
XLA Ops:
  1.9 67.1 %shard_map.68 = (f32[1024,128]{1,0:T(8,128)S(1)}, f32[2,1024,128]{2,1,0:T(8,128)S(1)}) custom-call(s32[1,1,1,1]{3,2,1,0:T(1,128)S(6)} %copy.7.brow_ref, s32[1,1,1]{2,1,0:T(1,128)S(6)} %copy.8.count_ref, f32[2,1024,128]{2,1,0:T(8,128)} %bitcast.3, bf16[4,8,1024]{2,1,0:T(8,128)(2,1)} %diag_hbm.1, bf16[1024,1024]{1,0:T(8,128)(2,1)} %bitcast.2), custom_call_target="tpu_custom_call" | custom-call | tf_op jit(solution)/shard_map/pallas_call | solution.py:536
  69.1 1.2 %shard_map.69 = (f32[1,1,1024,128]{3,2,1,0:T(8,128)}, f32[2,1,1024,128]{3,2,1,0:T(8,128)}) custom-call(f32[1024,128]{1,0:T(8,128)S(1)} %get-tuple-element.4.solved_in, f32[2,1024,128]{2,1,0:T(8,128)S(1)} %get-tuple-element.5.rem_in), custom_call_target="tpu_custom_call" | custom-call | tf_op jit(solution)/shard_map/pallas_call | solution.py:568
